TPU v7x, 32 devices: a whole 2x2x4 slice. The times are simulated.
32 devices in a mesh: space: 8 (over y, x, core), band: 4 (over z).
Axes of the slice: x: 2, y: 2, z: 4, core: 2. Of those that a mesh axis runs over, the one named last changes fastest.
Arguments:
- states_in: bfloat16 [256, 16384], P('band', 'space'), may hold values from -6 to 6
- kinetic: bfloat16 [64, 64], replicated, may hold values from -0.75 to 0.75
- cell_scale: float32 [2048], P('space'), may hold values from 0.5 to 2
- cell_nodes: int32 [64, 2048], P(None, 'space'), may hold values from 0 to 4095
- boundary: int32 [4096], P('space'), may hold values from 0 to 2047, as said below
- potential: float32 [16384], P('space'), may hold values from -2 to 2
- inv_mass_root: float32 [16384], P('space'), may hold values from 0.2 to 1.875
Outputs:
- filtered: bfloat16 [256, 16384], P('band', 'space')
- margin: float32 [256, 256], P('band')
Inputs may be any that keep to these rules, and one draw needn't show every extreme that they name: `boundary`: each partition's 512 entries are distinct node numbers of that partition. `cell_nodes`: A value below 2048 is a node of the cell's own partition; a value 2048 + j * 512 + b is entry b of the boundary list of the partition whose space index is the cell's own plus (-2, -1, 1, 2)[j], taken modulo the number of partitions.
All inputs are finite; a program needn't handle non-finite values.
Results may differ from a plain program's by a relative error of at most 0.0095.
Values may be sent and summed in bfloat16 or wider, within the bound.
A program may use at most 64 MiB of HBM per device.

v0:
```python
import jax
import jax.numpy as jnp
from jax import lax
from jax.sharding import PartitionSpec as P

OFFSETS = (-2, -1, 1, 2)
CENTER = 0.5
HALF = 6.0


def from_behind(x, axis, by):
    count = lax.axis_size(axis)
    return lax.ppermute(x, axis, [(i, (i + by) % count) for i in range(count)])


def apply_operator(values, kinetic, cell_nodes, cell_scale, potential, inv_root, boundary):
    owned_count = values.shape[1]
    rim_width = boundary.shape[0]
    state_rows = values.shape[0]
    scaled = (inv_root[None, :] * values.astype(jnp.float32)).astype(jnp.bfloat16)
    rim_values = jnp.take(scaled, boundary, axis=1)
    ext_pieces = [scaled]
    for offset in OFFSETS:
        ext_pieces.append(from_behind(rim_values, "space", -offset))
    extended = jnp.concatenate(ext_pieces, axis=1)
    gathered = jnp.take(extended, cell_nodes, axis=1)
    cell_terms = jnp.einsum("ij,sjc->sic", kinetic, gathered, preferred_element_type=jnp.float32)
    cell_terms = cell_terms * cell_scale[None, None, :]
    totals = jnp.zeros((state_rows, extended.shape[1]), jnp.float32)
    totals = totals.at[:, cell_nodes.reshape(-1)].add(cell_terms.reshape(state_rows, -1))
    result = totals[:, :owned_count]
    for slot_index, offset in enumerate(OFFSETS):
        lower = owned_count + slot_index * rim_width
        ghost_part = totals[:, lower : lower + rim_width]
        arrived = from_behind(ghost_part, "space", offset)
        result = result.at[:, boundary].add(arrived)
    return inv_root[None, :] * (result + potential[None, :] * scaled.astype(jnp.float32))


def inner_rows(left, right):
    return lax.dot_general(
        left,
        right,
        (((1,), (1,)), ((), ())),
        precision=lax.Precision.HIGHEST,
        preferred_element_type=jnp.float32,
    )


def body(states_in, kinetic, cell_scale, cell_nodes, boundary, potential, inv_mass_root):

    def operate(values):
        return apply_operator(
            values, kinetic, cell_nodes, cell_scale, potential, inv_mass_root, boundary
        )

    start_f = states_in.astype(jnp.float32)
    first = ((operate(states_in) - CENTER * start_f) / HALF).astype(jnp.bfloat16)
    second = 2.0 * (operate(first) - CENTER * first.astype(jnp.float32)) / HALF - start_f
    filtered = second.astype(jnp.bfloat16)
    node_total = states_in.shape[1] * lax.axis_size("space")
    regrouped = lax.all_to_all(
        second.astype(jnp.bfloat16), "band", split_axis=1, concat_axis=0, tiled=True
    ).astype(second.dtype)
    partial_sum = inner_rows(regrouped, regrouped)
    reduced = lax.psum_scatter(
        partial_sum.astype(jnp.bfloat16), "band", scatter_dimension=0, tiled=True
    ).astype(jnp.float32)
    mine = lax.psum(reduced, "space")
    return (filtered, mine / node_total)


def solution(mesh):
    in_specs = (
        P("band", "space"),
        P(),
        P("space"),
        P(None, "space"),
        P("space"),
        P("space"),
        P("space"),
    )
    out_specs = (P("band", "space"), P("band", None))
    return jax.shard_map(body, mesh=mesh, in_specs=in_specs, out_specs=out_specs, check_vma=False)
```

profile of v0, /device:TPU:0, one launch (start us, length us, event | category | flops | bytes accessed | tf_op | source)
XLA Modules:
  0.0 506.3 jit_solution(12194853524961475449)
XLA Ops:
  12.4 3.9 collective-permute-start.3
  18.4 7.1 %collective-permute-done = bf16[64,512]{0,1:T(8,128)(2,1)S(1)} collective-permute-done((bf16[64,512]{0,1:T(8,128)(2,1)S(1)}, bf16[64,512]{0,1:T(8,128)(2,1)S(1)}, u32[]{:S(2)}, u32[]{:S(2)}) %collective-permute-start) | collective-permute-done | bytes 65568 | tf_op jit(solution)/shard_map/ppermute | solution.py:13
  25.6 57.4 %gather_fusion.1 = bf16[16384,64]{1,0:T(8,128)(2,1)} fusion(bf16[64,4096]{0,1:T(8,128)(2,1)S(1)} %constant_dynamic-update-slice_fusion, s32[16384]{0:T(1024)S(1)} %broadcast_clamp_fusion), kind=kCustom, calls=%fused_computation.1.clone | custom fusion | bytes 4259840 | tf_op jit(solution)/shard_map/jit(_take)/gather | solution.py:26
  83.0 4.7 copy.16
  90.4 7.0 %copy.22 = f32[64,64,256]{0,2,1:T(8,128)} copy(f32[64,64,256]{2,1,0:T(8,128)} %multiply_bitcast_fusion.1) | data formatting | bytes 8388608 | tf_op jit(solution)/shard_map/reshape | solution.py:30
  97.4 88.1 %scatter_custom_fusion = f32[64,4096]{0,1:T(8,128)S(1)} fusion(s32[16384]{0:T(1024)} %bitcast.74, f32[16384,64]{1,0:T(8,128)} %bitcast.68, f32[]{:T(128)} %constant.24.clone.1), kind=kCustom, calls=%fused_computation.42 | custom fusion | flops 1048576 | bytes 1049088 | tf_op jit(solution)/shard_map/scatter-add | solution.py:30
  192.7 13.5 %collective-permute-done.4 = f32[64,512]{0,1:T(8,128)} collective-permute-done((f32[64,512]{0,1:T(8,128)S(1)}, f32[64,512]{0,1:T(8,128)}, u32[]{:S(2)}, u32[]{:S(2)}) %collective-permute-start.4) | collective-permute-done | bytes 131104 | tf_op jit(solution)/shard_map/ppermute | solution.py:13
  206.2 4.1 scatter_custom_fusion.1
  210.3 4.1 scatter_custom_fusion.2
  214.5 4.3 scatter_custom_fusion.3
  218.8 3.7 scatter_custom_fusion.4
  234.3 57.4 %gather_fusion.3 = bf16[16384,64]{1,0:T(8,128)(2,1)} fusion(bf16[64,4096]{0,1:T(8,128)(2,1)S(1)} %constant_dynamic-update-slice_fusion.5, s32[16384]{0:T(1024)S(1)} %broadcast_clamp_fusion), kind=kCustom, calls=%fused_computation.3.clone | custom fusion | bytes 4259840 | tf_op jit(solution)/shard_map/jit(_take)/gather | solution.py:26
  291.7 5.7 %copy.18 = bf16[64,256,64]{1,0,2:T(8,128)(2,1)} copy(bf16[64,256,64]{2,1,0:T(8,128)(2,1)} %bitcast.65) | data formatting | bytes 4194304 | tf_op jit(solution)/shard_map/jit(_take)/gather | solution.py:26
  297.4 4.3 multiply_bitcast_fusion
  301.7 7.0 %copy.23 = f32[64,64,256]{0,2,1:T(8,128)} copy(f32[64,64,256]{2,1,0:T(8,128)} %multiply_bitcast_fusion) | data formatting | bytes 8388608 | tf_op jit(solution)/shard_map/reshape | solution.py:30
  308.6 89.1 %scatter_custom_fusion.5 = f32[64,4096]{0,1:T(8,128)} fusion(s32[16384]{0:T(1024)} %bitcast.75, f32[16384,64]{1,0:T(8,128)} %bitcast.67, f32[]{:T(128)} %constant.24.clone.1), kind=kCustom, calls=%fused_computation.40 | custom fusion | flops 1048576 | bytes 1049088 | tf_op jit(solution)/shard_map/scatter-add | solution.py:30
  405.9 14.6 %collective-permute-done.12 = f32[64,512]{0,1:T(8,128)S(1)} collective-permute-done((f32[64,512]{0,1:T(8,128)S(1)}, f32[64,512]{0,1:T(8,128)S(1)}, u32[]{:S(2)}, u32[]{:S(2)}) %collective-permute-start.12) | collective-permute-done | bytes 131104 | tf_op jit(solution)/shard_map/ppermute | solution.py:13
  420.5 5.2 %scatter_custom_fusion.6 = f32[64,2048]{0,1:T(8,128)} fusion(f32[64,2048]{0,1:T(8,128)} %slice_add_fusion, s32[512]{0:T(512)S(1)} %compare_select_fusion.2, f32[64,512]{0,1:T(8,128)S(1)} %collective-permute-done.12), kind=kCustom, calls=%fused_computation.51 | custom fusion | flops 32768 | bytes 786432 | tf_op jit(solution)/shard_map/scatter-add | solution.py:36
  425.7 5.2 %scatter_custom_fusion.7 = f32[64,2048]{0,1:T(8,128)} fusion(f32[64,2048]{0,1:T(8,128)} %scatter_custom_fusion.6, s32[512]{0:T(512)S(1)} %compare_select_fusion.2, f32[64,512]{0,1:T(8,128)S(1)} %collective-permute-done.13), kind=kCustom, calls=%fused_computation.49 | custom fusion | flops 32768 | bytes 786432 | tf_op jit(solution)/shard_map/scatter-add | solution.py:36
  430.9 5.2 %scatter_custom_fusion.8 = f32[64,2048]{0,1:T(8,128)} fusion(f32[64,2048]{0,1:T(8,128)} %scatter_custom_fusion.7, s32[512]{0:T(512)S(1)} %compare_select_fusion.2, f32[64,512]{0,1:T(8,128)S(1)} %collective-permute-done.14), kind=kCustom, calls=%fused_computation.47 | custom fusion | flops 32768 | bytes 786432 | tf_op jit(solution)/shard_map/scatter-add | solution.py:36
  436.2 5.2 %scatter_custom_fusion.9 = f32[64,2048]{0,1:T(8,128)} fusion(f32[64,2048]{0,1:T(8,128)} %scatter_custom_fusion.8, s32[512]{0:T(512)S(1)} %compare_select_fusion.2, f32[64,512]{0,1:T(8,128)S(1)} %collective-permute-done.15), kind=kCustom, calls=%fused_computation.45 | custom fusion | flops 32768 | bytes 786432 | tf_op jit(solution)/shard_map/scatter-add | solution.py:36
  443.3 13.3 %all_to_all.19 = bf16[64,4,512]{2,0,1:T(8,128)(2,1)S(1)} all-to-all(bf16[64,4,512]{2,0,1:T(8,128)(2,1)S(1)} %copy.20), channel_id=1, replica_groups=mesh['space'=8,'band'=4] {'band'}, dimensions={1} | all-to-all | bytes 524288 | tf_op jit(solution)/shard_map/all_to_all | solution.py:62
  458.4 17.1 %reduce-scatter.2.cloned.1.call-done = bf16[64,256]{1,0:T(8,128)(2,1)} async-done(((bf16[256,256]{1,0:T(8,128)(2,1)}), bf16[64,256]{1,0:T(8,128)(2,1)}) %reduce-scatter.2.cloned.1.call-update) | async-done | bytes 32784 | tf_op jit(solution)/shard_map/reduce_scatter | solution.py:66
  475.5 23.3 %all-reduce.1 = f32[64,256]{1,0:T(8,128)S(1)} all-reduce(bf16[64,256]{1,0:T(8,128)(2,1)} %reduce-scatter.2.cloned.1.call-done), channel_id=1, replica_groups=mesh['space'=8,'band'=4] {'space'}, use_global_device_ids=true, to_apply=%region_11.14 | all-reduce | flops 16384 | bytes 98304 | tf_op jit(solution)/shard_map/psum | solution.py:69
  (78 shorter events, 41.6 us)
Async XLA Ops:
  7.2 80.6 %copy-start = (bf16[64,64]{1,0:T(8,128)(2,1)S(1)}, bf16[64,64]{1,0:T(8,128)(2,1)}, u32[]{:S(2)}) copy-start(bf16[64,64]{1,0:T(8,128)(2,1)} %param.12) | copy-start | bytes 24580
  7.2 10.4 %copy-start.3 = (s32[64,256]{1,0:T(8,128)S(1)}, s32[64,256]{1,0:T(8,128)}, u32[]{:S(2)}) copy-start(s32[64,256]{1,0:T(8,128)} %param.14) | copy-start | bytes 196612
  7.2 468.3 %reduce-scatter.2.cloned.1.call-start = ((), (), s32[]{:S(2)}) async-start(), calls=%async_computation.2 | async-start | bytes 163840 | tf_op jit(solution)/shard_map/reduce_scatter | solution.py:66
  12.4 13.2 %collective-permute-start.3 = (bf16[64,512]{0,1:T(8,128)(2,1)S(1)}, bf16[64,512]{0,1:T(8,128)(2,1)S(1)}, u32[]{:S(2)}, u32[]{:S(2)}) collective-permute-start(bf16[64,512]{0,1:T(8,128)(2,1)S(1)} %select_bitcast_fusion.1), channel_id=1, source_target_pairs={{0,24},{4,28},{8,0},{12,4},{16,8},{20,12},{24,16},{28,20},{1,25},{... | collective-permute-start | bytes 196616 | tf_op jit(solution)/shard_map/ppermute | solution.py:13
  16.3 9.2 %collective-permute-start.2 = (bf16[64,512]{0,1:T(8,128)(2,1)S(1)}, bf16[64,512]{0,1:T(8,128)(2,1)S(1)}, u32[]{:S(2)}, u32[]{:S(2)}) collective-permute-start(bf16[64,512]{0,1:T(8,128)(2,1)S(1)} %select_bitcast_fusion.1), channel_id=1, source_target_pairs={{0,28},{4,0},{8,4},{12,8},{16,12},{20,16},{24,20},{28,24},{1,29},{... | collective-permute-start | bytes 196616 | tf_op jit(solution)/shard_map/ppermute | solution.py:13
  16.3 9.2 %collective-permute-start.1 = (bf16[64,512]{0,1:T(8,128)(2,1)S(1)}, bf16[64,512]{0,1:T(8,128)(2,1)S(1)}, u32[]{:S(2)}, u32[]{:S(2)}) collective-permute-start(bf16[64,512]{0,1:T(8,128)(2,1)S(1)} %select_bitcast_fusion.1), channel_id=1, source_target_pairs={{0,4},{4,8},{8,12},{12,16},{16,20},{20,24},{24,28},{28,0},{1,5},{5... | collective-permute-start | bytes 196616 | tf_op jit(solution)/shard_map/ppermute | solution.py:13
  16.8 8.6 %collective-permute-start = (bf16[64,512]{0,1:T(8,128)(2,1)S(1)}, bf16[64,512]{0,1:T(8,128)(2,1)S(1)}, u32[]{:S(2)}, u32[]{:S(2)}) collective-permute-start(bf16[64,512]{0,1:T(8,128)(2,1)S(1)} %select_bitcast_fusion.1), channel_id=1, source_target_pairs={{0,8},{4,12},{8,16},{12,20},{16,24},{20,28},{24,0},{28,4},{1,9},{5... | collective-permute-start | bytes 196616 | tf_op jit(solution)/shard_map/ppermute | solution.py:13
  83.0 4.7 copy-start.6
  97.4 93.7 %copy-start.5 = (f32[2048]{0:T(1024)S(1)}, f32[2048]{0:T(1024)}, u32[]{:S(2)}) copy-start(f32[2048]{0:T(1024)} %param.16) | copy-start | bytes 24580
  185.5 5.3 %copy-start.2 = (f32[64,4096]{0,1:T(8,128)}, f32[64,4096]{0,1:T(8,128)S(1)}, u32[]{:S(2)}) copy-start(f32[64,4096]{0,1:T(8,128)S(1)} %scatter_custom_fusion) | copy-start | bytes 3145732
  186.5 32.3 %collective-permute-start.7 = (f32[64,512]{0,1:T(8,128)}, f32[64,512]{0,1:T(8,128)S(1)}, u32[]{:S(2)}, u32[]{:S(2)}) collective-permute-start(f32[64,512]{0,1:T(8,128)} %get-tuple-element.16), channel_id=1, source_target_pairs={{0,8},{4,12},{8,16},{12,20},{16,24},{20,28},{24,0},{28,4},{1,9},{5... | collective-permute-start | bytes 393224 | tf_op jit(solution)/shard_map/ppermute | solution.py:13
  188.2 26.3 %collective-permute-start.6 = (f32[64,512]{0,1:T(8,128)}, f32[64,512]{0,1:T(8,128)}, u32[]{:S(2)}, u32[]{:S(2)}) collective-permute-start(f32[64,512]{0,1:T(8,128)} %get-tuple-element.17), channel_id=1, source_target_pairs={{0,4},{4,8},{8,12},{12,16},{16,20},{20,24},{24,28},{28,0},{1,5},{5... | collective-permute-start | bytes 393224 | tf_op jit(solution)/shard_map/ppermute | solution.py:13
  188.2 22.2 %collective-permute-start.5 = (f32[64,512]{0,1:T(8,128)}, f32[64,512]{0,1:T(8,128)}, u32[]{:S(2)}, u32[]{:S(2)}) collective-permute-start(f32[64,512]{0,1:T(8,128)} %get-tuple-element.18), channel_id=1, source_target_pairs={{0,28},{4,0},{8,4},{12,8},{16,12},{20,16},{24,20},{28,24},{1,29},{... | collective-permute-start | bytes 393224 | tf_op jit(solution)/shard_map/ppermute | solution.py:13
  190.8 15.4 %collective-permute-start.4 = (f32[64,512]{0,1:T(8,128)S(1)}, f32[64,512]{0,1:T(8,128)}, u32[]{:S(2)}, u32[]{:S(2)}) collective-permute-start(f32[64,512]{0,1:T(8,128)S(1)} %get-tuple-element.19), channel_id=1, source_target_pairs={{0,24},{4,28},{8,0},{12,4},{16,8},{20,12},{24,16},{28,20},{1,25},{... | collective-permute-start | bytes 393224 | tf_op jit(solution)/shard_map/ppermute | solution.py:13
  210.3 12.2 %copy-start.4 = (f32[2048]{0:T(1024)S(1)}, f32[2048]{0:T(1024)}, u32[]{:S(2)}) copy-start(f32[2048]{0:T(1024)} %param.17) | copy-start | bytes 24580
  224.3 7.2 %collective-permute-start.8 = (bf16[64,512]{0,1:T(8,128)(2,1)S(1)}, bf16[64,512]{0,1:T(8,128)(2,1)S(1)}, u32[]{:S(2)}, u32[]{:S(2)}) collective-permute-start(bf16[64,512]{0,1:T(8,128)(2,1)S(1)} %select_bitcast_fusion), channel_id=1, source_target_pairs={{0,8},{4,12},{8,16},{12,20},{16,24},{20,28},{24,0},{28,4},{1,9},{5... | collective-permute-start | bytes 196616 | tf_op jit(solution)/shard_map/ppermute | solution.py:13
  225.1 9.2 %collective-permute-start.11 = (bf16[64,512]{0,1:T(8,128)(2,1)S(1)}, bf16[64,512]{0,1:T(8,128)(2,1)S(1)}, u32[]{:S(2)}, u32[]{:S(2)}) collective-permute-start(bf16[64,512]{0,1:T(8,128)(2,1)S(1)} %select_bitcast_fusion), channel_id=1, source_target_pairs={{0,24},{4,28},{8,0},{12,4},{16,8},{20,12},{24,16},{28,20},{1,25},{... | collective-permute-start | bytes 196616 | tf_op jit(solution)/shard_map/ppermute | solution.py:13
  227.3 6.8 %collective-permute-start.10 = (bf16[64,512]{0,1:T(8,128)(2,1)S(1)}, bf16[64,512]{0,1:T(8,128)(2,1)S(1)}, u32[]{:S(2)}, u32[]{:S(2)}) collective-permute-start(bf16[64,512]{0,1:T(8,128)(2,1)S(1)} %select_bitcast_fusion), channel_id=1, source_target_pairs={{0,28},{4,0},{8,4},{12,8},{16,12},{20,16},{24,20},{28,24},{1,29},{... | collective-permute-start | bytes 196616 | tf_op jit(solution)/shard_map/ppermute | solution.py:13
  227.3 6.8 %collective-permute-start.9 = (bf16[64,512]{0,1:T(8,128)(2,1)S(1)}, bf16[64,512]{0,1:T(8,128)(2,1)S(1)}, u32[]{:S(2)}, u32[]{:S(2)}) collective-permute-start(bf16[64,512]{0,1:T(8,128)(2,1)S(1)} %select_bitcast_fusion), channel_id=1, source_target_pairs={{0,4},{4,8},{8,12},{12,16},{16,20},{20,24},{24,28},{28,0},{1,5},{5... | collective-permute-start | bytes 196616 | tf_op jit(solution)/shard_map/ppermute | solution.py:13
  397.7 6.9 %copy-start.1 = (f32[64,4096]{0,1:T(8,128)S(1)}, f32[64,4096]{0,1:T(8,128)}, u32[]{:S(2)}) copy-start(f32[64,4096]{0,1:T(8,128)} %scatter_custom_fusion.5) | copy-start | bytes 3145732
  399.9 36.2 %collective-permute-start.15 = (f32[64,512]{0,1:T(8,128)S(1)}, f32[64,512]{0,1:T(8,128)S(1)}, u32[]{:S(2)}, u32[]{:S(2)}) collective-permute-start(f32[64,512]{0,1:T(8,128)S(1)} %get-tuple-element.12), channel_id=1, source_target_pairs={{0,8},{4,12},{8,16},{12,20},{16,24},{20,28},{24,0},{28,4},{1,9},{5... | collective-permute-start | bytes 393224 | tf_op jit(solution)/shard_map/ppermute | solution.py:13
  400.9 30.0 %collective-permute-start.14 = (f32[64,512]{0,1:T(8,128)}, f32[64,512]{0,1:T(8,128)S(1)}, u32[]{:S(2)}, u32[]{:S(2)}) collective-permute-start(f32[64,512]{0,1:T(8,128)} %get-tuple-element.13), channel_id=1, source_target_pairs={{0,4},{4,8},{8,12},{12,16},{16,20},{20,24},{24,28},{28,0},{1,5},{5... | collective-permute-start | bytes 393224 | tf_op jit(solution)/shard_map/ppermute | solution.py:13
  401.8 23.9 %collective-permute-start.13 = (f32[64,512]{0,1:T(8,128)}, f32[64,512]{0,1:T(8,128)S(1)}, u32[]{:S(2)}, u32[]{:S(2)}) collective-permute-start(f32[64,512]{0,1:T(8,128)} %get-tuple-element.14), channel_id=1, source_target_pairs={{0,28},{4,0},{8,4},{12,8},{16,12},{20,16},{24,20},{28,24},{1,29},{... | collective-permute-start | bytes 393224 | tf_op jit(solution)/shard_map/ppermute | solution.py:13
  403.5 17.0 %collective-permute-start.12 = (f32[64,512]{0,1:T(8,128)S(1)}, f32[64,512]{0,1:T(8,128)S(1)}, u32[]{:S(2)}, u32[]{:S(2)}) collective-permute-start(f32[64,512]{0,1:T(8,128)S(1)} %get-tuple-element.15), channel_id=1, source_target_pairs={{0,24},{4,28},{8,0},{12,4},{16,8},{20,12},{24,16},{28,20},{1,25},{... | collective-permute-start | bytes 393224 | tf_op jit(solution)/shard_map/ppermute | solution.py:13
Sparse Core Ops, SparseCore 0:
  457.6 17.8 reduce-scatter.1
where the time goes:
time: 507 us; the launch traced here: 506 us
  other arithmetic  223 us (44%)
  local copies, waits for them, and re-layouts  148 us (29%)
  waiting for transfers between devices  58.7 us (12%)
  blocking collectives  36.6 us (7%)
  starting transfers between devices  18 us (4%)
  between operations  14.4 us (3%)
  matrix products  7.85 us (2%)
    scatter-add x2, other arithmetic, apply_operator(): totals.at[:, cell_nodes.reshape(-1)].add(cell_terms.reshape(state_rows, -1))  177 us
    gather x4, local copies, waits for them, and re-layouts, apply_operator(): gathered = jnp.take(extended, cell_nodes, axis=1)  125 us
    ppermute x16, waiting for transfers between devices, from_behind(): return lax.ppermute(x, axis, [(i, (i + by) % count) for i in range(count)])  41.6 us
    scatter-add x8, other arithmetic, apply_operator(): result = result.at[:, boundary].add(arrived)  37 us
    psum x1, blocking collectives, body(): mine = lax.psum(reduced, 'space')  23.3 us
    ppermute x16, starting transfers between devices, from_behind(): return lax.ppermute(x, axis, [(i, (i + by) % count) for i in range(count)])  18 us
    reduce_scatter x1, waiting for transfers between devices, body(): lax.psum_scatter(partial_sum.astype(jnp.bfloat16), 'band', scatter_dimens...  17.1 us
    reshape x2, local copies, waits for them, and re-layouts, apply_operator(): cell_terms.reshape(state_rows, -1)  13.9 us
  transfers between devices with their start and end apart: 17, of which 7 were waited for; matrix products, arithmetic and copies ran while one was open for 6% of the time, Pallas kernels for 0%

commit v1 on v0

v1 whole, which is shorter than its diff:
```python
import functools

import jax
import jax.numpy as jnp
from jax import lax
from jax.experimental import pallas as pl
from jax.experimental.pallas import tpu as pltpu
from jax.sharding import PartitionSpec as P

OFFSETS = (-2, -1, 1, 2)
CENTER = 0.5
HALF = 6.0
LANES = 256
CHUNK = 16
F32 = jnp.float32
BF16 = jnp.bfloat16
NT = (((1,), (1,)), ((), ()))
VMEM = pl.BlockSpec(memory_space=pltpu.VMEM)


def from_behind(x, axis, by):
    count = lax.axis_size(axis)
    return lax.ppermute(x, axis, [(i, (i + by) % count) for i in range(count)])


def call(kernel, out_shape, *args, scratch=(), specs=None):
    return pl.pallas_call(
        kernel,
        out_shape=out_shape,
        in_specs=specs or [VMEM] * len(args),
        out_specs=jax.tree.map(lambda _: VMEM, out_shape),
        scratch_shapes=scratch,
        compiler_params=pltpu.CompilerParams(vmem_limit_bytes=56 * 2**20),
    )(*args)


def boundary_hot(boundary, nodes):
    shape = (nodes, boundary.shape[-1])
    return jnp.where(lax.broadcasted_iota(jnp.int32, shape, 0) == boundary, 1.0, 0.0).astype(BF16)


def scaled_of(values, inv_root):
    return (inv_root * values.astype(F32)).astype(BF16)


def pre_kernel(values, inv_root, boundary, scaled_out, rim_out):
    scaled = scaled_of(values[...], inv_root[...])
    scaled_out[...] = scaled
    hot = boundary_hot(boundary[...], scaled.shape[1])
    rim_out[...] = jnp.dot(scaled, hot, preferred_element_type=F32).astype(BF16)


def cells_kernel(scaled, g0, g1, g2, g3, nodes, nodes_row, scale, block, own_out, o0, o1, o2, o3, table, total):
    rows, owned = scaled.shape
    rim = g0.shape[1]
    parts = LANES // rows
    height = table.shape[1]
    shift = height.bit_length() - 1
    corners = nodes.shape[0]
    step = CHUNK * corners

    def place(at, width):
        return at // height * rows, at % height, min(width, height)

    for at in range(0, owned, height):
        row, col, width = place(at, owned)
        table[row : row + rows, col : col + width] = scaled[:, at : at + width]
    for slot, ghost in enumerate((g0, g1, g2, g3)):
        row, col, width = place(owned + slot * rim, rim)
        table[row : row + rows, col : col + width] = ghost[...]
    total[...] = jnp.zeros_like(total)
    weights = table[...]
    lane = lax.broadcasted_iota(jnp.int32, (corners, 128), 1)
    part_lane = lane // rows
    lane_b = lane.astype(F32).astype(BF16)

    def chunk(g, carry):
        base = g * CHUNK
        block_at = pl.multiple_of(base // 128 * 128, 128)
        ids = nodes[:, pl.ds(block_at, 128)]
        ids = pltpu.roll(ids, (128 - base % 128) % 128, axis=1)
        low = (ids & 127).astype(F32)
        high = ((ids >> 7) & (height // 128 - 1)).astype(F32)
        part = ids >> shift
        hots, masks = [], []
        for c in range(CHUNK):
            lo = jnp.broadcast_to(low[:, c : c + 1], (corners, 128)).astype(BF16)
            hi = jnp.broadcast_to(high[:, c : c + 1], (corners, 128)).astype(BF16)
            pt = jnp.broadcast_to(part[:, c : c + 1], (corners, 128))
            one = jnp.where(lo == lane_b, 1.0, 0.0).astype(BF16)
            hots.append(
                jnp.concatenate(
                    [jnp.where(hi == jnp.asarray(b, BF16), one, jnp.zeros_like(one)) for b in range(height // 128)],
                    axis=1,
                )
            )
            masks.append(
                jnp.concatenate([pt == part_lane + k * (128 // rows) for k in range(LANES // 128)], axis=1)
            )
        hot = jnp.concatenate(hots, axis=0)
        found = lax.dot_general(hot, weights, NT, preferred_element_type=F32)
        terms = []
        per = LANES // corners
        for q in range(0, CHUNK, per):
            picked = jnp.concatenate(
                [
                    jnp.where(masks[c], found[c * corners : (c + 1) * corners], 0.0).astype(BF16)
                    for c in range(q, q + per)
                ],
                axis=0,
            )
            term = jnp.dot(block[...], picked, preferred_element_type=F32)
            folded = term[:, :128]
            for k in range(128, LANES, 128):
                folded = folded + term[:, k : k + 128]
            spread = rows
            while spread < 128:
                folded = folded + pltpu.roll(folded, spread, axis=1)
                spread *= 2
            for c in range(q, q + per):
                mine = folded[(c - q) * corners : (c - q + 1) * corners] * scale[base + c]
                wide = jnp.concatenate([mine] * (LANES // 128), axis=1)
                terms.append(jnp.where(masks[c], wide, 0.0).astype(BF16))
        spread_terms = jnp.concatenate(terms, axis=0)
        row = (nodes_row[pl.ds(g, 1), :] & (height - 1))
        hot_t = jnp.where(
            lax.broadcasted_iota(jnp.int32, (height, step), 0) == row, 1.0, 0.0
        ).astype(BF16)
        total[...] += jnp.dot(hot_t, spread_terms, preferred_element_type=F32)
        return carry

    lax.fori_loop(0, nodes.shape[1] // CHUNK, chunk, 0)
    result = total[...].T
    for at in range(0, owned, height):
        row, col, width = place(at, owned)
        own_out[:, at : at + width] = result[row : row + rows, col : col + width]
    for slot, out in enumerate((o0, o1, o2, o3)):
        row, col, width = place(owned + slot * rim, rim)
        out[...] = result[row : row + rows, col : col + width].astype(out.dtype)


def gathered_total(own, arrived, hot, scaled, potential, inv_root):
    extra = sum(a[...].astype(F32) for a in arrived)
    added = lax.dot_general(extra.astype(BF16), hot, NT, preferred_element_type=F32)
    return inv_root * (own + added + potential * scaled.astype(F32))


def mid_kernel(values, scaled, own, a0, a1, a2, a3, potential, inv_root, boundary, first_out, scaled_out, rim_out):
    hot = boundary_hot(boundary[...], own.shape[1])
    image = gathered_total(own[...], (a0, a1, a2, a3), hot, scaled[...], potential[...], inv_root[...])
    first = ((image - CENTER * values[...].astype(F32)) * (1.0 / HALF)).astype(BF16)
    first_out[...] = first
    again = scaled_of(first, inv_root[...])
    scaled_out[...] = again
    rim_out[...] = jnp.dot(again, hot, preferred_element_type=F32).astype(BF16)


def post_kernel(start, first, scaled, own, a0, a1, a2, a3, potential, inv_root, boundary, second_out):
    hot = boundary_hot(boundary[...], own.shape[1])
    image = gathered_total(own[...], (a0, a1, a2, a3), hot, scaled[...], potential[...], inv_root[...])
    second = 2.0 * (image - CENTER * first[...].astype(F32)) * (1.0 / HALF) - start[...].astype(F32)
    second_out[...] = second.astype(BF16)


def body(states_in, kinetic, cell_scale, cell_nodes, boundary, potential, inv_mass_root):
    rows, owned = states_in.shape
    rim = boundary.shape[0]
    corners, cells = cell_nodes.shape
    height = (owned + len(OFFSETS) * rim) // (LANES // rows)
    per = LANES // corners
    block = jnp.kron(jnp.eye(per, dtype=BF16), kinetic)
    nodes_row = cell_nodes.T.reshape(cells // CHUNK, CHUNK * corners)
    edge = boundary[None, :]
    pot = potential[None, :]
    inv = inv_mass_root[None, :]
    field = jax.ShapeDtypeStruct((rows, owned), BF16)
    rim_shape = jax.ShapeDtypeStruct((rows, rim), BF16)

    def exchange(rim_values, scaled):
        ghosts = [from_behind(rim_values, "space", -offset) for offset in OFFSETS]
        own, *parts = call(
            cells_kernel,
            (jax.ShapeDtypeStruct((rows, owned), F32),) + (rim_shape,) * len(OFFSETS),
            scaled, *ghosts, cell_nodes, nodes_row, cell_scale, block,
            scratch=[pltpu.VMEM((LANES, height), BF16), pltpu.VMEM((height, LANES), F32)],
            specs=[VMEM] * 7 + [pl.BlockSpec(memory_space=pltpu.SMEM), VMEM],
        )
        return own, [from_behind(part, "space", offset) for part, offset in zip(parts, OFFSETS)]

    scaled, rim_values = call(pre_kernel, (field, rim_shape), states_in, inv, edge)
    own, arrived = exchange(rim_values, scaled)
    first, again, rim_values = call(
        mid_kernel, (field, field, rim_shape), states_in, scaled, own, *arrived, pot, inv, edge
    )
    own, arrived = exchange(rim_values, again)
    filtered = call(post_kernel, field, states_in, first, again, own, *arrived, pot, inv, edge)
    node_total = owned * lax.axis_size("space")
    regrouped = lax.all_to_all(filtered, "band", split_axis=1, concat_axis=0, tiled=True)
    partial_sum = lax.dot_general(regrouped, regrouped, NT, preferred_element_type=F32)
    reduced = lax.psum_scatter(partial_sum.astype(BF16), "band", scatter_dimension=0, tiled=True)
    mine = lax.psum(reduced.astype(F32), "space")
    return (filtered, mine / node_total)


def solution(mesh):
    in_specs = (
        P("band", "space"),
        P(),
        P("space"),
        P(None, "space"),
        P("space"),
        P("space"),
        P("space"),
    )
    out_specs = (P("band", "space"), P("band", None))
    return jax.shard_map(body, mesh=mesh, in_specs=in_specs, out_specs=out_specs, check_vma=False)
```

time: 507 us -> 202 us (0.40)
  other arithmetic: 223 us -> 0.81 us
  local copies, waits for them, and re-layouts: 148 us -> 5.81 us
  Pallas kernels: 0 us -> 94.7 us
  waiting for transfers between devices: 58.7 us -> 35.4 us
  matrix products: 7.85 us -> 0.9 us
    scatter-add x10 -> x0, other arithmetic: 214 us -> none  [the longest x2 177 us: apply_operator(): totals.at[:, cell_nodes.reshape(-1)].add(cell_terms.reshape(state_rows, -1))]
    gather x6 -> x0, local copies, waits for them, and re-layouts: 128 us -> none  [the longest x4 125 us: apply_operator(): gathered = jnp.take(extended, cell_nodes, axis=1)]
    pallas_call x0 -> x5, Pallas kernels: none -> 94.7 us  [call(): pl.pallas_call(kernel, out_shape=out_shape, in_specs=specs or [VMEM] * le...]
    ppermute x16, waiting for transfers between devices: 41.6 us -> 18.2 us  [from_behind(): return lax.ppermute(x, axis, [(i, (i + by) % count) for i in range(count)])]
    reshape x2 -> x1, local copies, waits for them, and re-layouts: 13.9 us -> 0.72 us  [body(): nodes_row = cell_nodes.T.reshape(cells // CHUNK, CHUNK * corners)]
    dot_general x3 -> x1, matrix products: 7.85 us -> 0.9 us  [body(): lax.dot_general(regrouped, regrouped, NT, preferred_element_type=F32)]
  transfers between devices with their start and end apart: 17 -> 17, of which waited for: 7 -> 13; matrix products, arithmetic and copies ran while one was open for 6% -> 1% of each run, Pallas kernels for 0% -> 0%
where the time goes in v1:
time: 202 us
  Pallas kernels  94.7 us (47%)
  blocking collectives  37.1 us (18%)
  waiting for transfers between devices  35.4 us (18%)
  between operations  14.1 us (7%)
  starting transfers between devices  13.1 us (6%)
  local copies, waits for them, and re-layouts  5.81 us (3%)
    pallas_call x5, Pallas kernels, call(): pl.pallas_call(kernel, out_shape=out_shape, in_specs=specs or [VMEM] * le...  94.7 us
    psum x1, blocking collectives, body(): mine = lax.psum(reduced.astype(F32), 'space')  23.3 us
    ppermute x16, waiting for transfers between devices, from_behind(): return lax.ppermute(x, axis, [(i, (i + by) % count) for i in range(count)])  18.2 us
    reduce_scatter x1, waiting for transfers between devices, body(): lax.psum_scatter(partial_sum.astype(BF16), 'band', scatter_dimension=0, t...  17.2 us
    all_to_all x1, blocking collectives, body(): lax.all_to_all(filtered, 'band', split_axis=1, concat_axis=0, tiled=True)  13.8 us
    ppermute x16, starting transfers between devices, from_behind(): return lax.ppermute(x, axis, [(i, (i + by) % count) for i in range(count)])  13.1 us
  transfers between devices with their start and end apart: 17, of which 13 were waited for; matrix products, arithmetic and copies ran while one was open for 1% of the time, Pallas kernels for 0%

profile of v1, /device:TPU:0, one launch (start us, length us, event | category | flops | bytes accessed | tf_op | source)
XLA Modules:
  0.0 202.1 jit_solution(16894596412670480156)
XLA Ops:
  7.2 2.1 %shard_map.86 = (bf16[64,2048]{1,0:T(8,128)(2,1)}, bf16[64,512]{1,0:T(8,128)(2,1)}) custom-call(bf16[64,2048]{1,0:T(8,128)(2,1)} %start.1, f32[1,2048]{1,0:T(1,128)} %bitcast.17, s32[1,512]{1,0:T(1,128)} %bitcast.22), custom_call_target="tpu_custom_call" | custom-call | tf_op jit(solution)/shard_map/pallas_call | solution.py:27
  9.3 3.9 %collective-permute-start.3 = (bf16[64,512]{1,0:T(8,128)(2,1)}, bf16[64,512]{1,0:T(8,128)(2,1)S(1)}, u32[]{:S(2)}, u32[]{:S(2)}) collective-permute-start(bf16[64,512]{1,0:T(8,128)(2,1)} %get-tuple-element.18), channel_id=1, source_target_pairs={{0,24},{4,28},{8,0},{12,4},{16,8},{20,12},{24,16},{28,20},{1,25},{... | collective-permute-start | bytes 196616 | tf_op jit(solution)/shard_map/ppermute | solution.py:23
  17.0 1.0 collective-permute-done.1.g1
  18.0 1.6 collective-permute-done.g0
  20.3 43.2 %shard_map.87 = (f32[64,2048]{1,0:T(8,128)}, bf16[64,512]{1,0:T(8,128)(2,1)}, bf16[64,512]{1,0:T(8,128)(2,1)}, bf16[64,512]{1,0:T(8,128)(2,1)}, bf16[64,512]{1,0:T(8,128)(2,1)}) custom-call(bf16[64,2048]{1,0:T(8,128)(2,1)} %get-tuple-element.17.scaled, bf16[64,512]{1,0:T(8,128)(2,1)} %copy-done.6, bf16[64,512]{1,0:T(8,128)(2,1)} %copy-done.3, ...), custom_call_target="tpu_custom_call" | custom-call | tf_op jit(solution)/shard_map/pallas_call | solution.py:27
  65.1 0.9 collective-permute-start.7
  66.0 1.9 collective-permute-done.4.a0
  67.9 2.1 %collective-permute-done.6.a2 = bf16[64,512]{1,0:T(8,128)(2,1)S(1)} collective-permute-done((bf16[64,512]{1,0:T(8,128)(2,1)}, bf16[64,512]{1,0:T(8,128)(2,1)S(1)}, u32[]{:S(2)}, u32[]{:S(2)}) %collective-permute-start.6) | collective-permute-done | bytes 65568 | tf_op jit(solution)/shard_map/ppermute | solution.py:23
  70.0 1.1 collective-permute-done.7.a3
  71.7 3.3 %shard_map.88 = (bf16[64,2048]{1,0:T(8,128)(2,1)}, bf16[64,2048]{1,0:T(8,128)(2,1)}, bf16[64,512]{1,0:T(8,128)(2,1)}) custom-call(bf16[64,2048]{1,0:T(8,128)(2,1)} %start.1, bf16[64,2048]{1,0:T(8,128)(2,1)} %get-tuple-element.17.scaled, f32[64,2048]{1,0:T(8,128)} %get-tuple-element.19.own, bf16[64,512]{1,0:T(8,128)(2,1)} %copy-done.13, ...), custom_call_target="tpu_custom_call" | custom-call | tf_op jit(solution)/shard_map/pallas_call | solution.py:27
  75.0 1.4 collective-permute-start.11
  77.9 1.6 collective-permute-done.11.g3
  79.8 2.3 %collective-permute-done.9.g1 = bf16[64,512]{1,0:T(8,128)(2,1)S(1)} collective-permute-done((bf16[64,512]{1,0:T(8,128)(2,1)}, bf16[64,512]{1,0:T(8,128)(2,1)S(1)}, u32[]{:S(2)}, u32[]{:S(2)}) %collective-permute-start.9) | collective-permute-done | bytes 65568 | tf_op jit(solution)/shard_map/ppermute | solution.py:23
  82.1 1.1 collective-permute-done.8.g0
  83.8 43.2 %shard_map.89 = (f32[64,2048]{1,0:T(8,128)}, bf16[64,512]{1,0:T(8,128)(2,1)}, bf16[64,512]{1,0:T(8,128)(2,1)}, bf16[64,512]{1,0:T(8,128)(2,1)}, bf16[64,512]{1,0:T(8,128)(2,1)}) custom-call(bf16[64,2048]{1,0:T(8,128)(2,1)} %get-tuple-element.25.scaled, bf16[64,512]{1,0:T(8,128)(2,1)} %copy-done.12, bf16[64,512]{1,0:T(8,128)(2,1)} %copy-done.10, ...), custom_call_target="tpu_custom_call" | custom-call | tf_op jit(solution)/shard_map/pallas_call | solution.py:27
  127.0 1.7 collective-permute-start.13
  129.6 1.9 collective-permute-done.12.a0
  131.5 2.2 %collective-permute-done.14.a2 = bf16[64,512]{1,0:T(8,128)(2,1)S(1)} collective-permute-done((bf16[64,512]{1,0:T(8,128)(2,1)}, bf16[64,512]{1,0:T(8,128)(2,1)S(1)}, u32[]{:S(2)}, u32[]{:S(2)}) %collective-permute-start.14) | collective-permute-done | bytes 65568 | tf_op jit(solution)/shard_map/ppermute | solution.py:23
  133.7 1.1 collective-permute-done.15.a3
  135.4 2.9 %shard_map.90 = bf16[64,2048]{1,0:T(8,128)(2,1)} custom-call(bf16[64,2048]{1,0:T(8,128)(2,1)} %start.1, bf16[64,2048]{1,0:T(8,128)(2,1)} %get-tuple-element.24.first, bf16[64,2048]{1,0:T(8,128)(2,1)} %get-tuple-element.25.scaled, f32[64,2048]{1,0:T(8,128)} %get-tuple-element.27.own, bf16[64,512]{1,0:T(8,128)(2,1)} %copy-done.4, bf16[64,512]{1,0:T(8,128)(2,1)} %copy-done.7, ...), custom_call_target="tpu_custom_call" | custom-call | tf_op jit(solution)/shard_map/pallas_call | solution.py:27
  138.3 1.0 copy.14
  139.3 13.8 %all_to_all.19 = bf16[64,4,512]{2,0,1:T(8,128)(2,1)S(1)} all-to-all(bf16[64,4,512]{2,0,1:T(8,128)(2,1)S(1)} %bitcast.14), channel_id=1, replica_groups=mesh['space'=8,'band'=4] {'band'}, dimensions={1} | all-to-all | bytes 524288 | tf_op jit(solution)/shard_map/all_to_all | solution.py:198
  154.1 17.2 %reduce-scatter.2.cloned.1.call-done = bf16[64,256]{1,0:T(8,128)(2,1)} async-done(((bf16[256,256]{1,0:T(8,128)(2,1)}), bf16[64,256]{1,0:T(8,128)(2,1)}) %reduce-scatter.2.cloned.1.call-update) | async-done | bytes 32784 | tf_op jit(solution)/shard_map/reduce_scatter | solution.py:200
  171.3 23.3 %all-reduce.1 = f32[64,256]{1,0:T(8,128)S(1)} all-reduce(bf16[64,256]{1,0:T(8,128)(2,1)} %reduce-scatter.2.cloned.1.call-done), channel_id=1, replica_groups=mesh['space'=8,'band'=4] {'space'}, use_global_device_ids=true, to_apply=%region_1.2 | all-reduce | flops 16384 | bytes 98304 | tf_op jit(solution)/shard_map/psum | solution.py:201
  (62 shorter events, 12.0 us)
Async XLA Ops:
  7.2 164.1 %reduce-scatter.2.cloned.1.call-start = ((), (), s32[]{:S(2)}) async-start(), calls=%async_computation.2 | async-start | bytes 163840 | tf_op jit(solution)/shard_map/reduce_scatter | solution.py:200
  7.2 7.2 %copy-start.17 = (bf16[64,64]{1,0:T(8,128)(2,1)S(1)}, bf16[64,64]{1,0:T(8,128)(2,1)}, u32[]{:S(2)}) copy-start(bf16[64,64]{1,0:T(8,128)(2,1)} %param.8) | copy-start | bytes 24580
  9.3 7.6 %collective-permute-start.3 = (bf16[64,512]{1,0:T(8,128)(2,1)}, bf16[64,512]{1,0:T(8,128)(2,1)S(1)}, u32[]{:S(2)}, u32[]{:S(2)}) collective-permute-start(bf16[64,512]{1,0:T(8,128)(2,1)} %get-tuple-element.18), channel_id=1, source_target_pairs={{0,24},{4,28},{8,0},{12,4},{16,8},{20,12},{24,16},{28,20},{1,25},{... | collective-permute-start | bytes 196616 | tf_op jit(solution)/shard_map/ppermute | solution.py:23
  13.2 3.8 %collective-permute-start.2 = (bf16[64,512]{1,0:T(8,128)(2,1)}, bf16[64,512]{1,0:T(8,128)(2,1)S(1)}, u32[]{:S(2)}, u32[]{:S(2)}) collective-permute-start(bf16[64,512]{1,0:T(8,128)(2,1)} %get-tuple-element.18), channel_id=1, source_target_pairs={{0,28},{4,0},{8,4},{12,8},{16,12},{20,16},{24,20},{28,24},{1,29},{... | collective-permute-start | bytes 196616 | tf_op jit(solution)/shard_map/ppermute | solution.py:23
  13.2 4.8 %collective-permute-start.1 = (bf16[64,512]{1,0:T(8,128)(2,1)}, bf16[64,512]{1,0:T(8,128)(2,1)S(1)}, u32[]{:S(2)}, u32[]{:S(2)}) collective-permute-start(bf16[64,512]{1,0:T(8,128)(2,1)} %get-tuple-element.18), channel_id=1, source_target_pairs={{0,4},{4,8},{8,12},{12,16},{16,20},{20,24},{24,28},{28,0},{1,5},{5... | collective-permute-start | bytes 196616 | tf_op jit(solution)/shard_map/ppermute | solution.py:23
  13.7 5.9 %collective-permute-start = (bf16[64,512]{1,0:T(8,128)(2,1)}, bf16[64,512]{1,0:T(8,128)(2,1)S(1)}, u32[]{:S(2)}, u32[]{:S(2)}) collective-permute-start(bf16[64,512]{1,0:T(8,128)(2,1)} %get-tuple-element.18), channel_id=1, source_target_pairs={{0,8},{4,12},{8,16},{12,20},{16,24},{20,28},{24,0},{28,4},{1,9},{5... | collective-permute-start | bytes 196616 | tf_op jit(solution)/shard_map/ppermute | solution.py:23
  63.5 4.5 %collective-permute-start.4 = (bf16[64,512]{1,0:T(8,128)(2,1)}, bf16[64,512]{1,0:T(8,128)(2,1)S(1)}, u32[]{:S(2)}, u32[]{:S(2)}) collective-permute-start(bf16[64,512]{1,0:T(8,128)(2,1)} %get-tuple-element.20), channel_id=1, source_target_pairs={{0,24},{4,28},{8,0},{12,4},{16,8},{20,12},{24,16},{28,20},{1,25},{... | collective-permute-start | bytes 196616 | tf_op jit(solution)/shard_map/ppermute | solution.py:23
  64.2 3.8 %collective-permute-start.5 = (bf16[64,512]{1,0:T(8,128)(2,1)}, bf16[64,512]{1,0:T(8,128)(2,1)S(1)}, u32[]{:S(2)}, u32[]{:S(2)}) collective-permute-start(bf16[64,512]{1,0:T(8,128)(2,1)} %get-tuple-element.21), channel_id=1, source_target_pairs={{0,28},{4,0},{8,4},{12,8},{16,12},{20,16},{24,20},{28,24},{1,29},{... | collective-permute-start | bytes 196616 | tf_op jit(solution)/shard_map/ppermute | solution.py:23
  65.0 4.9 %collective-permute-start.6 = (bf16[64,512]{1,0:T(8,128)(2,1)}, bf16[64,512]{1,0:T(8,128)(2,1)S(1)}, u32[]{:S(2)}, u32[]{:S(2)}) collective-permute-start(bf16[64,512]{1,0:T(8,128)(2,1)} %get-tuple-element.22), channel_id=1, source_target_pairs={{0,4},{4,8},{8,12},{12,16},{16,20},{20,24},{24,28},{28,0},{1,5},{5... | collective-permute-start | bytes 196616 | tf_op jit(solution)/shard_map/ppermute | solution.py:23
  65.1 6.0 %collective-permute-start.7 = (bf16[64,512]{1,0:T(8,128)(2,1)}, bf16[64,512]{1,0:T(8,128)(2,1)S(1)}, u32[]{:S(2)}, u32[]{:S(2)}) collective-permute-start(bf16[64,512]{1,0:T(8,128)(2,1)} %get-tuple-element.23), channel_id=1, source_target_pairs={{0,8},{4,12},{8,16},{12,20},{16,24},{20,28},{24,0},{28,4},{1,9},{5... | collective-permute-start | bytes 196616 | tf_op jit(solution)/shard_map/ppermute | solution.py:23
  67.9 3.2 %copy-start.13 = (bf16[64,512]{1,0:T(8,128)(2,1)}, bf16[64,512]{1,0:T(8,128)(2,1)S(1)}, u32[]{:S(2)}) copy-start(bf16[64,512]{1,0:T(8,128)(2,1)S(1)} %collective-permute-done.4.a0) | copy-start | bytes 196612
  67.9 3.2 %copy-start.14 = (bf16[64,512]{1,0:T(8,128)(2,1)}, bf16[64,512]{1,0:T(8,128)(2,1)S(1)}, u32[]{:S(2)}) copy-start(bf16[64,512]{1,0:T(8,128)(2,1)S(1)} %collective-permute-done.5.a1) | copy-start | bytes 196612
  75.0 4.5 %collective-permute-start.11 = (bf16[64,512]{1,0:T(8,128)(2,1)}, bf16[64,512]{1,0:T(8,128)(2,1)S(1)}, u32[]{:S(2)}, u32[]{:S(2)}) collective-permute-start(bf16[64,512]{1,0:T(8,128)(2,1)} %get-tuple-element.26), channel_id=1, source_target_pairs={{0,24},{4,28},{8,0},{12,4},{16,8},{20,12},{24,16},{28,20},{1,25},{... | collective-permute-start | bytes 196616 | tf_op jit(solution)/shard_map/ppermute | solution.py:23
  76.4 3.3 %collective-permute-start.10 = (bf16[64,512]{1,0:T(8,128)(2,1)}, bf16[64,512]{1,0:T(8,128)(2,1)S(1)}, u32[]{:S(2)}, u32[]{:S(2)}) collective-permute-start(bf16[64,512]{1,0:T(8,128)(2,1)} %get-tuple-element.26), channel_id=1, source_target_pairs={{0,28},{4,0},{8,4},{12,8},{16,12},{20,16},{24,20},{28,24},{1,29},{... | collective-permute-start | bytes 196616 | tf_op jit(solution)/shard_map/ppermute | solution.py:23
  77.1 4.9 %collective-permute-start.9 = (bf16[64,512]{1,0:T(8,128)(2,1)}, bf16[64,512]{1,0:T(8,128)(2,1)S(1)}, u32[]{:S(2)}, u32[]{:S(2)}) collective-permute-start(bf16[64,512]{1,0:T(8,128)(2,1)} %get-tuple-element.26), channel_id=1, source_target_pairs={{0,4},{4,8},{8,12},{12,16},{16,20},{20,24},{24,28},{28,0},{1,5},{5... | collective-permute-start | bytes 196616 | tf_op jit(solution)/shard_map/ppermute | solution.py:23
  77.1 6.0 %collective-permute-start.8 = (bf16[64,512]{1,0:T(8,128)(2,1)}, bf16[64,512]{1,0:T(8,128)(2,1)S(1)}, u32[]{:S(2)}, u32[]{:S(2)}) collective-permute-start(bf16[64,512]{1,0:T(8,128)(2,1)} %get-tuple-element.26), channel_id=1, source_target_pairs={{0,8},{4,12},{8,16},{12,20},{16,24},{20,28},{24,0},{28,4},{1,9},{5... | collective-permute-start | bytes 196616 | tf_op jit(solution)/shard_map/ppermute | solution.py:23
  79.5 3.7 %copy-start.5 = (bf16[64,512]{1,0:T(8,128)(2,1)}, bf16[64,512]{1,0:T(8,128)(2,1)S(1)}, u32[]{:S(2)}) copy-start(bf16[64,512]{1,0:T(8,128)(2,1)S(1)} %collective-permute-done.11.g3) | copy-start | bytes 196612
  79.8 3.4 %copy-start.8 = (bf16[64,512]{1,0:T(8,128)(2,1)}, bf16[64,512]{1,0:T(8,128)(2,1)S(1)}, u32[]{:S(2)}) copy-start(bf16[64,512]{1,0:T(8,128)(2,1)S(1)} %collective-permute-done.10.g2) | copy-start | bytes 196612
  127.0 4.5 %collective-permute-start.12 = (bf16[64,512]{1,0:T(8,128)(2,1)}, bf16[64,512]{1,0:T(8,128)(2,1)S(1)}, u32[]{:S(2)}, u32[]{:S(2)}) collective-permute-start(bf16[64,512]{1,0:T(8,128)(2,1)} %get-tuple-element.28), channel_id=1, source_target_pairs={{0,24},{4,28},{8,0},{12,4},{16,8},{20,12},{24,16},{28,20},{1,25},{... | collective-permute-start | bytes 196616 | tf_op jit(solution)/shard_map/ppermute | solution.py:23
  127.0 4.5 %collective-permute-start.13 = (bf16[64,512]{1,0:T(8,128)(2,1)}, bf16[64,512]{1,0:T(8,128)(2,1)S(1)}, u32[]{:S(2)}, u32[]{:S(2)}) collective-permute-start(bf16[64,512]{1,0:T(8,128)(2,1)} %get-tuple-element.29), channel_id=1, source_target_pairs={{0,28},{4,0},{8,4},{12,8},{16,12},{20,16},{24,20},{28,24},{1,29},{... | collective-permute-start | bytes 196616 | tf_op jit(solution)/shard_map/ppermute | solution.py:23
  128.7 4.9 %collective-permute-start.14 = (bf16[64,512]{1,0:T(8,128)(2,1)}, bf16[64,512]{1,0:T(8,128)(2,1)S(1)}, u32[]{:S(2)}, u32[]{:S(2)}) collective-permute-start(bf16[64,512]{1,0:T(8,128)(2,1)} %get-tuple-element.30), channel_id=1, source_target_pairs={{0,4},{4,8},{8,12},{12,16},{16,20},{20,24},{24,28},{28,0},{1,5},{5... | collective-permute-start | bytes 196616 | tf_op jit(solution)/shard_map/ppermute | solution.py:23
  128.7 6.0 %collective-permute-start.15 = (bf16[64,512]{1,0:T(8,128)(2,1)}, bf16[64,512]{1,0:T(8,128)(2,1)S(1)}, u32[]{:S(2)}, u32[]{:S(2)}) collective-permute-start(bf16[64,512]{1,0:T(8,128)(2,1)} %get-tuple-element.31), channel_id=1, source_target_pairs={{0,8},{4,12},{8,16},{12,20},{16,24},{20,28},{24,0},{28,4},{1,9},{5... | collective-permute-start | bytes 196616 | tf_op jit(solution)/shard_map/ppermute | solution.py:23
  131.5 3.3 %copy-start.4 = (bf16[64,512]{1,0:T(8,128)(2,1)}, bf16[64,512]{1,0:T(8,128)(2,1)S(1)}, u32[]{:S(2)}) copy-start(bf16[64,512]{1,0:T(8,128)(2,1)S(1)} %collective-permute-done.12.a0) | copy-start | bytes 196612
  131.5 3.3 %copy-start.7 = (bf16[64,512]{1,0:T(8,128)(2,1)}, bf16[64,512]{1,0:T(8,128)(2,1)S(1)}, u32[]{:S(2)}) copy-start(bf16[64,512]{1,0:T(8,128)(2,1)S(1)} %collective-permute-done.13.a1) | copy-start | bytes 196612
  (11 other events, 13.6 us)
Sparse Core Ops, SparseCore 0:
  154.2 17.0 reduce-scatter.1

commit v2 on v1

v2 whole, which is shorter than its diff:
```python
import jax
import jax.numpy as jnp
from jax import lax
from jax.experimental import pallas as pl
from jax.experimental.pallas import tpu as pltpu
from jax.sharding import PartitionSpec as P

OFFSETS = (-2, -1, 1, 2)
CENTER = 0.5
HALF = 6.0
LANES = 256
CHUNK = 16
F32 = jnp.float32
BF16 = jnp.bfloat16
MESH = pl.DeviceIdType.MESH
NT = (((1,), (1,)), ((), ()))


def scaled_of(values, inv_root):
    return (inv_root * values.astype(F32)).astype(BF16)


def place(at, width, height, rows):
    return at // height * rows, at % height, min(width, height)


def apply_cells(scaled, ghosts, nodes, nodes_row, scale, block, table, total):
    rows, owned = scaled.shape
    rim = ghosts.shape[-1]
    height = table.shape[1]
    shift = height.bit_length() - 1
    corners = nodes.shape[0]
    step = CHUNK * corners
    for at in range(0, owned, height):
        row, col, width = place(at, owned, height, rows)
        table[row : row + rows, col : col + width] = scaled[:, at : at + width]
    for slot in range(len(OFFSETS)):
        row, col, width = place(owned + slot * rim, rim, height, rows)
        table[row : row + rows, col : col + width] = ghosts[slot]
    total[...] = jnp.zeros_like(total)
    part_lane = lax.broadcasted_iota(jnp.int32, (corners, 128), 1) // rows
    lane_b = lax.broadcasted_iota(jnp.int32, (corners, 128), 1).astype(F32).astype(BF16)
    high_count = height // 128

    def chunk(g, carry):
        base = g * CHUNK
        block_at = pl.multiple_of(base // 128 * 128, 128)
        ids = nodes[:, pl.ds(block_at, 128)]
        ids = pltpu.roll(ids, lax.rem(128 - lax.rem(base, 128), 128), axis=1)
        low = (ids & 127).astype(F32)
        high = ((ids >> 7) & (high_count - 1)).astype(F32)
        part = ids >> shift
        hots, masks = [], []
        for c in range(CHUNK):
            lo = jnp.broadcast_to(low[:, c : c + 1], (corners, 128)).astype(BF16)
            hi = jnp.broadcast_to(high[:, c : c + 1], (corners, 128)).astype(BF16)
            pt = jnp.broadcast_to(part[:, c : c + 1], (corners, 128))
            one = jnp.where(lo == lane_b, 1.0, 0.0).astype(BF16)
            hots.append(
                jnp.concatenate(
                    [jnp.where(hi == jnp.asarray(b, BF16), one, jnp.zeros_like(one)) for b in range(high_count)],
                    axis=1,
                )
            )
            masks.append(
                jnp.concatenate([pt == part_lane + k * (128 // rows) for k in range(LANES // 128)], axis=1)
            )
        hot = jnp.concatenate(hots, axis=0)
        found = lax.dot_general(hot, table[...], NT, preferred_element_type=F32)

        row = nodes_row[pl.ds(g, 1), :]
        low_row = jnp.broadcast_to((row & 127).astype(F32), (16, step)).astype(BF16)
        high_row = jnp.broadcast_to(((row >> 7) & (high_count - 1)).astype(F32), (16, step)).astype(BF16)
        sub = lax.broadcasted_iota(jnp.int32, (16, step), 0)
        ones_t = [
            jnp.where(low_row == (sub + s).astype(F32).astype(BF16), 1.0, 0.0).astype(BF16)
            for s in range(0, 128, 16)
        ]
        hots_t = []
        for b in range(high_count):
            here = high_row == jnp.asarray(b, BF16)
            hots_t += [jnp.where(here, one, jnp.zeros_like(one)) for one in ones_t]
        hot_t = jnp.concatenate(hots_t, axis=0)

        terms = []
        per = LANES // corners
        for q in range(0, CHUNK, per):
            picked = jnp.concatenate(
                [
                    jnp.where(masks[c], found[c * corners : (c + 1) * corners], 0.0).astype(BF16)
                    for c in range(q, q + per)
                ],
                axis=0,
            )
            term = jnp.dot(block[...], picked, preferred_element_type=F32)
            folded = term[:, :128]
            for k in range(128, LANES, 128):
                folded = folded + term[:, k : k + 128]
            spread = rows
            while spread < 128:
                folded = folded + pltpu.roll(folded, spread, axis=1)
                spread *= 2
            for c in range(q, q + per):
                mine = folded[(c - q) * corners : (c - q + 1) * corners] * scale[base + c]
                wide = jnp.concatenate([mine] * (LANES // 128), axis=1)
                terms.append(jnp.where(masks[c], wide, 0.0).astype(BF16))
        total[...] += jnp.dot(hot_t, jnp.concatenate(terms, axis=0), preferred_element_type=F32)
        return carry

    lax.fori_loop(0, nodes.shape[1] // CHUNK, chunk, 0)


def kernel(
    n_space, n_band,
    start, block, scale, nodes, nodes_row, edge, potential, inv_root,
    filtered, margin,
    hot, scaled, first, table, total, rims, ghosts, parts, back, quarters, gram, gram_in, gathered,
    rim_send, rim_recv, part_send, part_recv, quarter_send, quarter_recv, gram_send, gram_recv, row_send, row_recv,
):
    p, b = lax.axis_index("space"), lax.axis_index("band")
    space_at = [(lax.rem(p + k, n_space), b) for k in range(n_space)]
    band_at = [(p, lax.rem(b + k, n_band)) for k in range(n_band)]
    barrier = pltpu.get_barrier_semaphore()
    for device in space_at[1:] + band_at[1:]:
        pl.semaphore_signal(barrier, inc=1, device_id=device, device_id_type=MESH)

    def remote(src, dst, send, recv, device):
        copy = pltpu.make_async_remote_copy(
            src_ref=src, dst_ref=dst, send_sem=send, recv_sem=recv, device_id=device, device_id_type=MESH
        )
        copy.start()
        return copy

    rows, owned = start.shape
    rim = edge.shape[-1]
    height = table.shape[1]
    node_at = lax.broadcasted_iota(jnp.int32, (owned, rim), 0)
    hot[...] = jnp.where(node_at == edge[...], 1.0, 0.0).astype(BF16)

    def operate(turn, values):
        scaled[...] = scaled_of(values, inv_root[...])
        rims[turn] = jnp.dot(scaled[...], hot[...], preferred_element_type=F32).astype(BF16)
        if turn == 0:
            pl.semaphore_wait(barrier, n_space + n_band - 2)
        sent = [
            remote(
                rims.at[turn], ghosts.at[turn, slot], rim_send.at[turn, slot], rim_recv.at[turn, slot],
                space_at[-offset % n_space],
            )
            for slot, offset in enumerate(OFFSETS)
        ]
        for copy in sent:
            copy.wait()
        apply_cells(scaled, ghosts.at[turn], nodes, nodes_row, scale, block, table, total)
        sent = []
        for slot, offset in enumerate(OFFSETS):
            row, col, width = place(owned + slot * rim, rim, height, rows)
            parts[turn, slot] = total[col : col + width, row : row + rows].T.astype(BF16)
            sent.append(
                remote(
                    parts.at[turn, slot], back.at[turn, slot], part_send.at[turn, slot], part_recv.at[turn, slot],
                    space_at[offset % n_space],
                )
            )
        own = []
        for at in range(0, owned, height):
            row, col, width = place(at, owned, height, rows)
            own.append(total[col : col + width, row : row + rows].T)
        own = jnp.concatenate(own, axis=1) + potential[...] * scaled[...].astype(F32)
        for copy in sent:
            copy.wait()
        extra = sum(back[turn, slot].astype(F32) for slot in range(len(OFFSETS))).astype(BF16)
        added = lax.dot_general(extra, hot[...], NT, preferred_element_type=F32)
        return inv_root[...] * (own + added)

    image = operate(0, start[...])
    first[...] = ((image - CENTER * start[...].astype(F32)) / HALF).astype(BF16)
    image = operate(1, first[...])
    second = 2.0 * (image - CENTER * first[...].astype(F32)) / HALF - start[...].astype(F32)
    filtered[...] = second.astype(BF16)

    share = owned // n_band
    sent = []
    for k in range(1, n_band):
        at = pl.multiple_of(band_at[k][1] * share, share)
        sent.append(
            remote(
                filtered.at[:, pl.ds(at, share)], quarters.at[b], quarter_send.at[k], quarter_recv.at[k], band_at[k]
            )
        )
    quarters[b] = filtered[:, pl.ds(pl.multiple_of(b * share, share), share)]
    for copy in sent:
        copy.wait()
    states = quarters[...].reshape(n_band * rows, share)
    gram[...] = (
        lax.dot_general(states, states, NT, preferred_element_type=F32).astype(BF16).reshape(gram.shape)
    )
    sent = [
        remote(gram.at[band_at[k][1]], gram_in.at[b], gram_send.at[k], gram_recv.at[k], band_at[k])
        for k in range(1, n_band)
    ]
    gram_in[b] = gram[b]
    for copy in sent:
        copy.wait()
    gathered[p] = sum(gram_in[k].astype(F32) for k in range(n_band)).astype(BF16)
    sent = [
        remote(gathered.at[p], gathered.at[p], row_send.at[k], row_recv.at[k], space_at[k])
        for k in range(1, n_space)
    ]
    for copy in sent:
        copy.wait()
    margin[...] = sum(gathered[k].astype(F32) for k in range(n_space)) / (owned * n_space)


def body(n_space, n_band, states_in, kinetic, cell_scale, cell_nodes, boundary, potential, inv_mass_root):
    rows, owned = states_in.shape
    rim = boundary.shape[0]
    corners, cells = cell_nodes.shape
    slots = len(OFFSETS)
    height = (owned + slots * rim) // (LANES // rows)
    block = jnp.kron(jnp.eye(LANES // corners, dtype=BF16), kinetic)
    nodes_row = cell_nodes.T.reshape(cells // CHUNK, CHUNK * corners)
    vmem = pl.BlockSpec(memory_space=pltpu.VMEM)
    smem = pl.BlockSpec(memory_space=pltpu.SMEM)
    states = n_band * rows

    def run(*refs):
        kernel(n_space, n_band, *refs)

    return pl.pallas_call(
        run,
        out_shape=(
            jax.ShapeDtypeStruct((rows, owned), BF16),
            jax.ShapeDtypeStruct((rows, states), F32),
        ),
        in_specs=[vmem, vmem, smem] + [vmem] * 5,
        out_specs=(vmem, vmem),
        scratch_shapes=[
            pltpu.VMEM((owned, rim), BF16),
            pltpu.VMEM((rows, owned), BF16),
            pltpu.VMEM((rows, owned), BF16),
            pltpu.VMEM((LANES, height), BF16),
            pltpu.VMEM((height, LANES), F32),
            pltpu.VMEM((2, rows, rim), BF16),
            pltpu.VMEM((2, slots, rows, rim), BF16),
            pltpu.VMEM((2, slots, rows, rim), BF16),
            pltpu.VMEM((2, slots, rows, rim), BF16),
            pltpu.VMEM((n_band, rows, owned // n_band), BF16),
            pltpu.VMEM((n_band, rows, states), BF16),
            pltpu.VMEM((n_band, rows, states), BF16),
            pltpu.VMEM((n_space, rows, states), BF16),
        ]
        + [pltpu.SemaphoreType.DMA((2, slots))] * 4
        + [pltpu.SemaphoreType.DMA((n_band,))] * 4
        + [pltpu.SemaphoreType.DMA((n_space,))] * 2,
        compiler_params=pltpu.CompilerParams(
            collective_id=0, has_side_effects=True, vmem_limit_bytes=56 * 2**20
        ),
    )(
        states_in, block, cell_scale, cell_nodes, nodes_row,
        boundary[None, :], potential[None, :], inv_mass_root[None, :],
    )


def solution(mesh):
    n_space, n_band = mesh.shape["space"], mesh.shape["band"]
    in_specs = (
        P("band", "space"),
        P(),
        P("space"),
        P(None, "space"),
        P("space"),
        P("space"),
        P("space"),
    )
    out_specs = (P("band", "space"), P("band", None))

    def run(*args):
        return body(n_space, n_band, *args)

    return jax.shard_map(run, mesh=mesh, in_specs=in_specs, out_specs=out_specs, check_vma=False)
```

time: 202 us -> 136 us (0.67)
  blocking collectives: 37.1 us -> 0 us
  waiting for transfers between devices: 35.4 us -> 0 us
  Pallas kernels: 94.7 us -> 130 us
  between operations: 14.1 us -> 0.67 us
  starting transfers between devices: 13.1 us -> 0 us
    pallas_call x5 -> x1, Pallas kernels: 94.7 us -> 130 us  [body(): pl.pallas_call(run, out_shape=(jax.ShapeDtypeStruct((rows, owned), BF16),...]
    psum x1 -> x0, blocking collectives: 23.3 us -> none  [body(): mine = lax.psum(reduced.astype(F32), 'space')]
    ppermute x16 -> x0, waiting for transfers between devices: 18.2 us -> none  [from_behind(): return lax.ppermute(x, axis, [(i, (i + by) % count) for i in range(count)])]
    reduce_scatter x1 -> x0, waiting for transfers between devices: 17.2 us -> none  [body(): lax.psum_scatter(partial_sum.astype(BF16), 'band', scatter_dimension=0, t...]
    all_to_all x1 -> x0, blocking collectives: 13.8 us -> none  [body(): lax.all_to_all(filtered, 'band', split_axis=1, concat_axis=0, tiled=True)]
    ppermute x16 -> x0, starting transfers between devices: 13.1 us -> none  [from_behind(): return lax.ppermute(x, axis, [(i, (i + by) % count) for i in range(count)])]
  transfers between devices with their start and end apart: 17 -> 0, of which waited for: 13 -> 0; matrix products, arithmetic and copies ran while one was open for 1% -> 0% of each run, Pallas kernels for 0% -> 0%
where the time goes in v2:
time: 136 us; the launch traced here: 135 us
  Pallas kernels  130 us (96%)
  local copies, waits for them, and re-layouts  4.87 us (4%)
    pallas_call x1, Pallas kernels, body(): pl.pallas_call(run, out_shape=(jax.ShapeDtypeStruct((rows, owned), BF16),...  130 us

profile of v2, /device:TPU:0, one launch (start us, length us, event | category | flops | bytes accessed | tf_op | source)
XLA Modules:
  0.0 135.4 jit_solution(13988663092040078313)
XLA Ops:
  0.6 0.9 copy.10
  1.6 0.0 copy-start.1
  1.6 0.7 reshape.21.refs_4_
  2.3 0.0 copy-done.1
  2.3 0.2 broadcast_multiply_fusion
  2.5 0.9 mul.27.refs_1_
  3.4 129.7 %shard_map.86 = (bf16[64,2048]{1,0:T(8,128)(2,1)}, f32[64,256]{1,0:T(8,128)}) custom-call(bf16[64,2048]{1,0:T(8,128)(2,1)} %refs_0_.1, bf16[256,256]{1,0:T(8,128)(2,1)} %mul.27.refs_1_, f32[256]{0:T(256)} %refs_2_.1, s32[64,256]{1,0:T(8,128)} %refs_3_.1, s32[16,1024]{1,0:T(8,128)} %reshape.21.refs_4_, s32[1,512]{1,0:T(1,128)} %bitcast.7, f32[1,2048]{1,0:T(1,128)} %bitcast.5, ...), custom_call_target="tpu_custom_call" | custom-call | tf_op jit(solution)/shard_map/pallas_call | solution.py:230
  133.1 0.0 copy-start
  133.1 1.7 %copy.13 = bf16[64,2048]{1,0:T(8,128)(2,1)} copy(bf16[64,2048]{1,0:T(8,128)(2,1)} %get-tuple-element.4) | data formatting | bytes 524288
  134.8 0.0 copy-done
  134.8 0.6 copy.14
  (1 shorter events, 0.0 us)
Async XLA Ops:
  1.6 0.7 copy-start.1
  133.1 1.7 %copy-start = (f32[64,256]{1,0:T(8,128)S(1)}, f32[64,256]{1,0:T(8,128)}, u32[]{:S(2)}) copy-start(f32[64,256]{1,0:T(8,128)} %get-tuple-element.5) | copy-start | bytes 196612

commit v3 on v2

--- a/solution.py
+++ b/solution.py
@@ -24,7 +24,7 @@
     return at // height * rows, at % height, min(width, height)
 
 
-def apply_cells(scaled, ghosts, nodes, nodes_row, scale, block, table, total):
+def apply_cells(scaled, ghosts, nodes, nodes_row, scale, block, table, turned, total):
     rows, owned = scaled.shape
     rim = ghosts.shape[-1]
     height = table.shape[1]
@@ -37,8 +37,12 @@
     for slot in range(len(OFFSETS)):
         row, col, width = place(owned + slot * rim, rim, height, rows)
         table[row : row + rows, col : col + width] = ghosts[slot]
+    turned[...] = table[...].astype(F32).T.astype(BF16)
     total[...] = jnp.zeros_like(total)
-    part_lane = lax.broadcasted_iota(jnp.int32, (corners, 128), 1) // rows
+    part_lane = [
+        ((lax.broadcasted_iota(jnp.int32, (corners, 128), 1) + k) // rows).astype(F32).astype(BF16)
+        for k in range(0, LANES, 128)
+    ]
     lane_b = lax.broadcasted_iota(jnp.int32, (corners, 128), 1).astype(F32).astype(BF16)
     high_count = height // 128
 
@@ -49,12 +53,12 @@
         ids = pltpu.roll(ids, lax.rem(128 - lax.rem(base, 128), 128), axis=1)
         low = (ids & 127).astype(F32)
         high = ((ids >> 7) & (high_count - 1)).astype(F32)
-        part = ids >> shift
+        part = (ids >> shift).astype(F32)
         hots, masks = [], []
         for c in range(CHUNK):
             lo = jnp.broadcast_to(low[:, c : c + 1], (corners, 128)).astype(BF16)
             hi = jnp.broadcast_to(high[:, c : c + 1], (corners, 128)).astype(BF16)
-            pt = jnp.broadcast_to(part[:, c : c + 1], (corners, 128))
+            pt = jnp.broadcast_to(part[:, c : c + 1], (corners, 128)).astype(BF16)
             one = jnp.where(lo == lane_b, 1.0, 0.0).astype(BF16)
             hots.append(
                 jnp.concatenate(
@@ -63,10 +67,10 @@
                 )
             )
             masks.append(
-                jnp.concatenate([pt == part_lane + k * (128 // rows) for k in range(LANES // 128)], axis=1)
+                jnp.concatenate([jnp.where(pt == lanes, 1.0, 0.0).astype(BF16) for lanes in part_lane], axis=1)
             )
         hot = jnp.concatenate(hots, axis=0)
-        found = lax.dot_general(hot, table[...], NT, preferred_element_type=F32)
+        found = jnp.dot(hot, turned[...], preferred_element_type=F32)
 
         row = nodes_row[pl.ds(g, 1), :]
         low_row = jnp.broadcast_to((row & 127).astype(F32), (16, step)).astype(BF16)
@@ -87,7 +91,7 @@
         for q in range(0, CHUNK, per):
             picked = jnp.concatenate(
                 [
-                    jnp.where(masks[c], found[c * corners : (c + 1) * corners], 0.0).astype(BF16)
+                    found[c * corners : (c + 1) * corners].astype(BF16) * masks[c]
                     for c in range(q, q + per)
                 ],
                 axis=0,
@@ -101,9 +105,8 @@
                 folded = folded + pltpu.roll(folded, spread, axis=1)
                 spread *= 2
             for c in range(q, q + per):
-                mine = folded[(c - q) * corners : (c - q + 1) * corners] * scale[base + c]
-                wide = jnp.concatenate([mine] * (LANES // 128), axis=1)
-                terms.append(jnp.where(masks[c], wide, 0.0).astype(BF16))
+                mine = (folded[(c - q) * corners : (c - q + 1) * corners] * scale[base + c]).astype(BF16)
+                terms.append(jnp.concatenate([mine] * (LANES // 128), axis=1) * masks[c])
         total[...] += jnp.dot(hot_t, jnp.concatenate(terms, axis=0), preferred_element_type=F32)
         return carry
 
@@ -112,9 +115,9 @@
 
 def kernel(
     n_space, n_band,
-    start, block, scale, nodes, nodes_row, edge, potential, inv_root,
+    start, kinetic, scale, nodes, nodes_row, edge, potential, inv_root,
     filtered, margin,
-    hot, scaled, first, table, total, rims, ghosts, parts, back, quarters, gram, gram_in, gathered,
+    hot, scaled, first, table, turned, total, block, rims, ghosts, parts, back, quarters, gram, gram_in, gathered,
     rim_send, rim_recv, part_send, part_recv, quarter_send, quarter_recv, gram_send, gram_recv, row_send, row_recv,
 ):
     p, b = lax.axis_index("space"), lax.axis_index("band")
@@ -134,6 +137,11 @@
     rows, owned = start.shape
     rim = edge.shape[-1]
     height = table.shape[1]
+    corners = kinetic.shape[0]
+    tiled = jnp.concatenate([kinetic[...].astype(F32)] * (LANES // corners), axis=0)
+    tiled = jnp.concatenate([tiled] * (LANES // corners), axis=1)
+    group = [lax.broadcasted_iota(jnp.int32, (LANES, LANES), axis) // corners for axis in (0, 1)]
+    block[...] = jnp.where(group[0] == group[1], tiled, 0.0).astype(BF16)
     node_at = lax.broadcasted_iota(jnp.int32, (owned, rim), 0)
     hot[...] = jnp.where(node_at == edge[...], 1.0, 0.0).astype(BF16)
 
@@ -151,22 +159,27 @@
         ]
         for copy in sent:
             copy.wait()
-        apply_cells(scaled, ghosts.at[turn], nodes, nodes_row, scale, block, table, total)
+        apply_cells(scaled, ghosts.at[turn], nodes, nodes_row, scale, block, table, turned, total)
+        flipped = {}
+
+        def piece(at, length):
+            row, col, width = place(at, length, height, rows)
+            column = row // 128 * 128
+            if column not in flipped:
+                flipped[column] = total[:, column : column + 128].T
+            return flipped[column][row - column : row - column + rows, col : col + width]
+
         sent = []
         for slot, offset in enumerate(OFFSETS):
-            row, col, width = place(owned + slot * rim, rim, height, rows)
-            parts[turn, slot] = total[col : col + width, row : row + rows].T.astype(BF16)
+            parts[turn, slot] = piece(owned + slot * rim, rim).astype(BF16)
             sent.append(
                 remote(
                     parts.at[turn, slot], back.at[turn, slot], part_send.at[turn, slot], part_recv.at[turn, slot],
                     space_at[offset % n_space],
                 )
             )
-        own = []
-        for at in range(0, owned, height):
-            row, col, width = place(at, owned, height, rows)
-            own.append(total[col : col + width, row : row + rows].T)
-        own = jnp.concatenate(own, axis=1) + potential[...] * scaled[...].astype(F32)
+        own = jnp.concatenate([piece(at, owned) for at in range(0, owned, height)], axis=1)
+        own = own + potential[...] * scaled[...].astype(F32)
         for copy in sent:
             copy.wait()
         extra = sum(back[turn, slot].astype(F32) for slot in range(len(OFFSETS))).astype(BF16)
@@ -218,7 +231,6 @@
     corners, cells = cell_nodes.shape
     slots = len(OFFSETS)
     height = (owned + slots * rim) // (LANES // rows)
-    block = jnp.kron(jnp.eye(LANES // corners, dtype=BF16), kinetic)
     nodes_row = cell_nodes.T.reshape(cells // CHUNK, CHUNK * corners)
     vmem = pl.BlockSpec(memory_space=pltpu.VMEM)
     smem = pl.BlockSpec(memory_space=pltpu.SMEM)
@@ -240,7 +252,9 @@
             pltpu.VMEM((rows, owned), BF16),
             pltpu.VMEM((rows, owned), BF16),
             pltpu.VMEM((LANES, height), BF16),
+            pltpu.VMEM((height, LANES), BF16),
             pltpu.VMEM((height, LANES), F32),
+            pltpu.VMEM((LANES, LANES), BF16),
             pltpu.VMEM((2, rows, rim), BF16),
             pltpu.VMEM((2, slots, rows, rim), BF16),
             pltpu.VMEM((2, slots, rows, rim), BF16),
@@ -257,7 +271,7 @@
             collective_id=0, has_side_effects=True, vmem_limit_bytes=56 * 2**20
         ),
     )(
-        states_in, block, cell_scale, cell_nodes, nodes_row,
+        states_in, kinetic, cell_scale, cell_nodes, nodes_row,
         boundary[None, :], potential[None, :], inv_mass_root[None, :],
     )
 

time: 136 us -> 134 us (0.985)
  no operation moved by 1% of the time
where the time goes in v3:
time: 134 us
  Pallas kernels  130 us (97%)
  local copies, waits for them, and re-layouts  4 us (3%)
    pallas_call x1, Pallas kernels, body(): pl.pallas_call(run, out_shape=(jax.ShapeDtypeStruct((rows, owned), BF16),...  130 us

profile of v3, /device:TPU:0, one launch (start us, length us, event | category | flops | bytes accessed | tf_op | source)
XLA Modules:
  0.0 134.3 jit_solution(8052886406960912925)
XLA Ops:
  0.6 0.9 copy.10
  1.6 0.7 reshape.7.refs_4_
  2.3 129.6 %shard_map.86 = (bf16[64,2048]{1,0:T(8,128)(2,1)}, f32[64,256]{1,0:T(8,128)}) custom-call(bf16[64,2048]{1,0:T(8,128)(2,1)} %refs_0_.1, bf16[64,64]{1,0:T(8,128)(2,1)} %refs_1_.1, f32[256]{0:T(256)} %refs_2_.1, s32[64,256]{1,0:T(8,128)} %refs_3_.1, s32[16,1024]{1,0:T(8,128)} %reshape.7.refs_4_, s32[1,512]{1,0:T(1,128)} %bitcast.7, f32[1,2048]{1,0:T(1,128)} %bitcast.5, ...), custom_call_target="tpu_custom_call" | custom-call | tf_op jit(solution)/shard_map/pallas_call | solution.py:242
  131.9 0.0 copy-start
  131.9 1.7 %copy.13 = bf16[64,2048]{1,0:T(8,128)(2,1)} copy(bf16[64,2048]{1,0:T(8,128)(2,1)} %get-tuple-element.4) | data formatting | bytes 524288
  133.6 0.0 copy-done
  133.6 0.6 copy.14
Async XLA Ops:
  131.9 1.7 %copy-start = (f32[64,256]{1,0:T(8,128)S(1)}, f32[64,256]{1,0:T(8,128)}, u32[]{:S(2)}) copy-start(f32[64,256]{1,0:T(8,128)} %get-tuple-element.5) | copy-start | bytes 196612

commit v4 on v3

--- a/solution.py
+++ b/solution.py
@@ -8,7 +8,8 @@
 OFFSETS = (-2, -1, 1, 2)
 CENTER = 0.5
 HALF = 6.0
-LANES = 256
+LANES = 512
+DEPTH = 256
 CHUNK = 16
 F32 = jnp.float32
 BF16 = jnp.bfloat16
@@ -86,27 +87,28 @@
             hots_t += [jnp.where(here, one, jnp.zeros_like(one)) for one in ones_t]
         hot_t = jnp.concatenate(hots_t, axis=0)
 
-        terms = []
-        per = LANES // corners
-        for q in range(0, CHUNK, per):
-            picked = jnp.concatenate(
-                [
-                    found[c * corners : (c + 1) * corners].astype(BF16) * masks[c]
-                    for c in range(q, q + per)
-                ],
-                axis=0,
-            )
-            term = jnp.dot(block[...], picked, preferred_element_type=F32)
-            folded = term[:, :128]
-            for k in range(128, LANES, 128):
-                folded = folded + term[:, k : k + 128]
-            spread = rows
-            while spread < 128:
-                folded = folded + pltpu.roll(folded, spread, axis=1)
-                spread *= 2
-            for c in range(q, q + per):
-                mine = (folded[(c - q) * corners : (c - q + 1) * corners] * scale[base + c]).astype(BF16)
-                terms.append(jnp.concatenate([mine] * (LANES // 128), axis=1) * masks[c])
+        per = DEPTH // corners
+        picked = []
+        for c in range(CHUNK):
+            wide = found[c * corners : (c + 1) * corners].astype(BF16) * masks[c]
+            picked.append(sum(wide[:, k : k + 128] for k in range(128, LANES, 128)) + wide[:, :128])
+        left = lax.broadcasted_iota(jnp.int32, (corners, 128), 1) < rows
+        pairs = [(at + cell, at + per + cell) for at in range(0, CHUNK, 2 * per) for cell in range(per)]
+        tiles = []
+        for one, two in pairs:
+            first, other = picked[one].astype(F32), picked[two].astype(F32)
+            crossed = pltpu.roll(jnp.where(left, other, first), rows, axis=1)
+            tiles.append((jnp.where(left, first, other) + crossed).astype(BF16))
+        columns = [jnp.concatenate(tiles[at : at + per], axis=0) for at in range(0, len(tiles), per)]
+        term = jnp.dot(block[...], jnp.concatenate(columns, axis=1), preferred_element_type=F32)
+        terms = [None] * CHUNK
+        for k, (one, two) in enumerate(pairs):
+            cell, column = k % per, k // per * 128
+            tile = term[cell * corners : (cell + 1) * corners, column : column + 128]
+            tile = tile * jnp.where(left, scale[base + one], scale[base + two])
+            crossed = pltpu.roll(tile, rows, axis=1)
+            for at, both in ((one, jnp.where(left, tile, crossed)), (two, jnp.where(left, crossed, tile))):
+                terms[at] = jnp.concatenate([both.astype(BF16)] * (LANES // 128), axis=1) * masks[at]
         total[...] += jnp.dot(hot_t, jnp.concatenate(terms, axis=0), preferred_element_type=F32)
         return carry
 
@@ -138,9 +140,9 @@
     rim = edge.shape[-1]
     height = table.shape[1]
     corners = kinetic.shape[0]
-    tiled = jnp.concatenate([kinetic[...].astype(F32)] * (LANES // corners), axis=0)
-    tiled = jnp.concatenate([tiled] * (LANES // corners), axis=1)
-    group = [lax.broadcasted_iota(jnp.int32, (LANES, LANES), axis) // corners for axis in (0, 1)]
+    tiled = jnp.concatenate([kinetic[...].astype(F32)] * (DEPTH // corners), axis=0)
+    tiled = jnp.concatenate([tiled] * (DEPTH // corners), axis=1)
+    group = [lax.broadcasted_iota(jnp.int32, (DEPTH, DEPTH), axis) // corners for axis in (0, 1)]
     block[...] = jnp.where(group[0] == group[1], tiled, 0.0).astype(BF16)
     node_at = lax.broadcasted_iota(jnp.int32, (owned, rim), 0)
     hot[...] = jnp.where(node_at == edge[...], 1.0, 0.0).astype(BF16)
@@ -254,7 +256,7 @@
             pltpu.VMEM((LANES, height), BF16),
             pltpu.VMEM((height, LANES), BF16),
             pltpu.VMEM((height, LANES), F32),
-            pltpu.VMEM((LANES, LANES), BF16),
+            pltpu.VMEM((DEPTH, DEPTH), BF16),
             pltpu.VMEM((2, rows, rim), BF16),
             pltpu.VMEM((2, slots, rows, rim), BF16),
             pltpu.VMEM((2, slots, rows, rim), BF16),

time: 134 us -> 124 us (0.925)
  Pallas kernels: 130 us -> 119 us
    pallas_call x1, Pallas kernels: 130 us -> 119 us  [body(): pl.pallas_call(run, out_shape=(jax.ShapeDtypeStruct((rows, owned), BF16),...]
where the time goes in v4:
time: 124 us; the launch traced here: 123 us
  Pallas kernels  119 us (96%)
  local copies, waits for them, and re-layouts  4 us (3%)
    pallas_call x1, Pallas kernels, body(): pl.pallas_call(run, out_shape=(jax.ShapeDtypeStruct((rows, owned), BF16),...  119 us

profile of v4, /device:TPU:0, one launch (start us, length us, event | category | flops | bytes accessed | tf_op | source)
XLA Modules:
  0.0 123.4 jit_solution(6136214268081949668)
XLA Ops:
  0.6 0.9 copy.10
  1.6 0.7 reshape.7.refs_4_
  2.3 118.8 %shard_map.86 = (bf16[64,2048]{1,0:T(8,128)(2,1)}, f32[64,256]{1,0:T(8,128)}) custom-call(bf16[64,2048]{1,0:T(8,128)(2,1)} %refs_0_.1, bf16[64,64]{1,0:T(8,128)(2,1)} %refs_1_.1, f32[256]{0:T(256)} %refs_2_.1, s32[64,256]{1,0:T(8,128)} %refs_3_.1, s32[16,1024]{1,0:T(8,128)} %reshape.7.refs_4_, s32[1,512]{1,0:T(1,128)} %bitcast.7, f32[1,2048]{1,0:T(1,128)} %bitcast.5, ...), custom_call_target="tpu_custom_call" | custom-call | tf_op jit(solution)/shard_map/pallas_call | solution.py:244
  121.1 0.0 copy-start
  121.1 1.7 %copy.13 = bf16[64,2048]{1,0:T(8,128)(2,1)} copy(bf16[64,2048]{1,0:T(8,128)(2,1)} %get-tuple-element.4) | data formatting | bytes 524288
  122.8 0.0 copy-done
  122.8 0.6 copy.14
Async XLA Ops:
  121.1 1.7 %copy-start = (f32[64,256]{1,0:T(8,128)S(1)}, f32[64,256]{1,0:T(8,128)}, u32[]{:S(2)}) copy-start(f32[64,256]{1,0:T(8,128)} %get-tuple-element.5) | copy-start | bytes 196612

commit v5 on v4

--- a/solution.py
+++ b/solution.py
@@ -25,26 +25,12 @@
     return at // height * rows, at % height, min(width, height)
 
 
-def apply_cells(scaled, ghosts, nodes, nodes_row, scale, block, table, turned, total):
-    rows, owned = scaled.shape
-    rim = ghosts.shape[-1]
-    height = table.shape[1]
+def build_hots(nodes, nodes_row, hots, hots_t, part_of, height):
     shift = height.bit_length() - 1
     corners = nodes.shape[0]
     step = CHUNK * corners
-    for at in range(0, owned, height):
-        row, col, width = place(at, owned, height, rows)
-        table[row : row + rows, col : col + width] = scaled[:, at : at + width]
-    for slot in range(len(OFFSETS)):
-        row, col, width = place(owned + slot * rim, rim, height, rows)
-        table[row : row + rows, col : col + width] = ghosts[slot]
-    turned[...] = table[...].astype(F32).T.astype(BF16)
-    total[...] = jnp.zeros_like(total)
-    part_lane = [
-        ((lax.broadcasted_iota(jnp.int32, (corners, 128), 1) + k) // rows).astype(F32).astype(BF16)
-        for k in range(0, LANES, 128)
-    ]
     lane_b = lax.broadcasted_iota(jnp.int32, (corners, 128), 1).astype(F32).astype(BF16)
+    sub = lax.broadcasted_iota(jnp.int32, (16, step), 0)
     high_count = height // 128
 
     def chunk(g, carry):
@@ -55,71 +41,98 @@
         low = (ids & 127).astype(F32)
         high = ((ids >> 7) & (high_count - 1)).astype(F32)
         part = (ids >> shift).astype(F32)
-        hots, masks = [], []
         for c in range(CHUNK):
+            at = pl.ds(c * corners, corners)
             lo = jnp.broadcast_to(low[:, c : c + 1], (corners, 128)).astype(BF16)
             hi = jnp.broadcast_to(high[:, c : c + 1], (corners, 128)).astype(BF16)
-            pt = jnp.broadcast_to(part[:, c : c + 1], (corners, 128)).astype(BF16)
+            part_of[g, at, :] = jnp.broadcast_to(part[:, c : c + 1], (corners, 128)).astype(BF16)
             one = jnp.where(lo == lane_b, 1.0, 0.0).astype(BF16)
-            hots.append(
-                jnp.concatenate(
-                    [jnp.where(hi == jnp.asarray(b, BF16), one, jnp.zeros_like(one)) for b in range(high_count)],
-                    axis=1,
-                )
-            )
-            masks.append(
-                jnp.concatenate([jnp.where(pt == lanes, 1.0, 0.0).astype(BF16) for lanes in part_lane], axis=1)
-            )
-        hot = jnp.concatenate(hots, axis=0)
-        found = jnp.dot(hot, turned[...], preferred_element_type=F32)
-
+            for b in range(high_count):
+                hots[g, at, b * 128 : (b + 1) * 128] = jnp.where(hi == jnp.asarray(b, BF16), one, jnp.zeros_like(one))
         row = nodes_row[pl.ds(g, 1), :]
         low_row = jnp.broadcast_to((row & 127).astype(F32), (16, step)).astype(BF16)
         high_row = jnp.broadcast_to(((row >> 7) & (high_count - 1)).astype(F32), (16, step)).astype(BF16)
-        sub = lax.broadcasted_iota(jnp.int32, (16, step), 0)
-        ones_t = [
-            jnp.where(low_row == (sub + s).astype(F32).astype(BF16), 1.0, 0.0).astype(BF16)
-            for s in range(0, 128, 16)
-        ]
-        hots_t = []
-        for b in range(high_count):
-            here = high_row == jnp.asarray(b, BF16)
-            hots_t += [jnp.where(here, one, jnp.zeros_like(one)) for one in ones_t]
-        hot_t = jnp.concatenate(hots_t, axis=0)
-
-        per = DEPTH // corners
-        picked = []
-        for c in range(CHUNK):
-            wide = found[c * corners : (c + 1) * corners].astype(BF16) * masks[c]
-            picked.append(sum(wide[:, k : k + 128] for k in range(128, LANES, 128)) + wide[:, :128])
-        left = lax.broadcasted_iota(jnp.int32, (corners, 128), 1) < rows
-        pairs = [(at + cell, at + per + cell) for at in range(0, CHUNK, 2 * per) for cell in range(per)]
+        here = [high_row == jnp.asarray(b, BF16) for b in range(high_count)]
+        for s in range(0, 128, 16):
+            one = jnp.where(low_row == (sub + s).astype(F32).astype(BF16), 1.0, 0.0).astype(BF16)
+            for b in range(high_count):
+                hots_t[g, b * 128 + s : b * 128 + s + 16, :] = jnp.where(here[b], one, jnp.zeros_like(one))
+        return carry
+
+    lax.fori_loop(0, hots.shape[0], chunk, 0)
+
+
+def apply_cells(scaled, ghosts, hots, hots_t, part_of, scale, block, table, turned, spread, total):
+    rows, owned = scaled.shape
+    rim = ghosts.shape[-1]
+    height = table.shape[1]
+    corners = hots.shape[1] // CHUNK
+    count = hots.shape[0]
+    for at in range(0, owned, height):
+        row, col, width = place(at, owned, height, rows)
+        table[row : row + rows, col : col + width] = scaled[:, at : at + width]
+    for slot in range(len(OFFSETS)):
+        row, col, width = place(owned + slot * rim, rim, height, rows)
+        table[row : row + rows, col : col + width] = ghosts[slot]
+    turned[...] = table[...].astype(F32).T.astype(BF16)
+    lane = lax.broadcasted_iota(jnp.int32, (corners, 128), 1)
+    part_lane = [((lane + k) // rows).astype(F32).astype(BF16) for k in range(0, LANES, 128)]
+    left = lane < rows
+    per = DEPTH // corners
+    pairs = [(at + cell, at + per + cell) for at in range(0, CHUNK, 2 * per) for cell in range(per)]
+
+    def find(g):
+        return jnp.dot(hots[g], turned[...], preferred_element_type=F32)
+
+    def add(g):
+        total[...] += jnp.dot(hots_t[g], spread[...], preferred_element_type=F32)
+
+    def apply(g, found):
+        base = g * CHUNK
+
+        def mask(c):
+            part = part_of[g, c * corners : (c + 1) * corners, :]
+            return [jnp.where(part == lanes, 1.0, 0.0).astype(BF16) for lanes in part_lane]
+
+        def pick(c):
+            wide = found[c * corners : (c + 1) * corners].astype(BF16)
+            return sum(wide[:, k * 128 : (k + 1) * 128] * m for k, m in enumerate(mask(c))).astype(F32)
+
         tiles = []
         for one, two in pairs:
-            first, other = picked[one].astype(F32), picked[two].astype(F32)
+            first, other = pick(one), pick(two)
             crossed = pltpu.roll(jnp.where(left, other, first), rows, axis=1)
             tiles.append((jnp.where(left, first, other) + crossed).astype(BF16))
         columns = [jnp.concatenate(tiles[at : at + per], axis=0) for at in range(0, len(tiles), per)]
         term = jnp.dot(block[...], jnp.concatenate(columns, axis=1), preferred_element_type=F32)
-        terms = [None] * CHUNK
         for k, (one, two) in enumerate(pairs):
             cell, column = k % per, k // per * 128
             tile = term[cell * corners : (cell + 1) * corners, column : column + 128]
             tile = tile * jnp.where(left, scale[base + one], scale[base + two])
             crossed = pltpu.roll(tile, rows, axis=1)
             for at, both in ((one, jnp.where(left, tile, crossed)), (two, jnp.where(left, crossed, tile))):
-                terms[at] = jnp.concatenate([both.astype(BF16)] * (LANES // 128), axis=1) * masks[at]
-        total[...] += jnp.dot(hot_t, jnp.concatenate(terms, axis=0), preferred_element_type=F32)
+                narrow = both.astype(BF16)
+                for n, m in enumerate(mask(at)):
+                    spread[at * corners : (at + 1) * corners, n * 128 : (n + 1) * 128] = narrow * m
+
+    total[...] = jnp.zeros_like(total)
+    apply(0, find(0))
+
+    def chunk(g, carry):
+        found = find(g)
+        add(g - 1)
+        apply(g, found)
         return carry
 
-    lax.fori_loop(0, nodes.shape[1] // CHUNK, chunk, 0)
+    lax.fori_loop(1, count, chunk, 0)
+    add(count - 1)
 
 
 def kernel(
     n_space, n_band,
     start, kinetic, scale, nodes, nodes_row, edge, potential, inv_root,
     filtered, margin,
-    hot, scaled, first, table, turned, total, block, rims, ghosts, parts, back, quarters, gram, gram_in, gathered,
+    hot, scaled, first, table, turned, total, block, hots, hots_t, part_of, spread, rims, ghosts, parts, back, quarters, gram, gram_in, gathered,
     rim_send, rim_recv, part_send, part_recv, quarter_send, quarter_recv, gram_send, gram_recv, row_send, row_recv,
 ):
     p, b = lax.axis_index("space"), lax.axis_index("band")
@@ -159,9 +172,13 @@
             )
             for slot, offset in enumerate(OFFSETS)
         ]
+        if turn == 0:
+            build_hots(nodes, nodes_row, hots, hots_t, part_of, height)
         for copy in sent:
             copy.wait()
-        apply_cells(scaled, ghosts.at[turn], nodes, nodes_row, scale, block, table, turned, total)
+        apply_cells(
+            scaled, ghosts.at[turn], hots, hots_t, part_of, scale, block, table, turned, spread, total
+        )
         flipped = {}
 
         def piece(at, length):
@@ -233,7 +250,8 @@
     corners, cells = cell_nodes.shape
     slots = len(OFFSETS)
     height = (owned + slots * rim) // (LANES // rows)
-    nodes_row = cell_nodes.T.reshape(cells // CHUNK, CHUNK * corners)
+    count, step = cells // CHUNK, CHUNK * corners
+    nodes_row = cell_nodes.T.reshape(count, step)
     vmem = pl.BlockSpec(memory_space=pltpu.VMEM)
     smem = pl.BlockSpec(memory_space=pltpu.SMEM)
     states = n_band * rows
@@ -257,6 +275,10 @@
             pltpu.VMEM((height, LANES), BF16),
             pltpu.VMEM((height, LANES), F32),
             pltpu.VMEM((DEPTH, DEPTH), BF16),
+            pltpu.VMEM((count, step, height), BF16),
+            pltpu.VMEM((count, height, step), BF16),
+            pltpu.VMEM((count, step, 128), BF16),
+            pltpu.VMEM((step, LANES), BF16),
             pltpu.VMEM((2, rows, rim), BF16),
             pltpu.VMEM((2, slots, rows, rim), BF16),
             pltpu.VMEM((2, slots, rows, rim), BF16),

time: 124 us -> 120 us (0.968)
  Pallas kernels: 119 us -> 115 us
    pallas_call x1, Pallas kernels: 119 us -> 115 us  [body(): pl.pallas_call(run, out_shape=(jax.ShapeDtypeStruct((rows, owned), BF16),...]
where the time goes in v5:
time: 120 us
  Pallas kernels  115 us (96%)
  local copies, waits for them, and re-layouts  4 us (3%)
    pallas_call x1, Pallas kernels, body(): pl.pallas_call(run, out_shape=(jax.ShapeDtypeStruct((rows, owned), BF16),...  115 us

profile of v5, /device:TPU:0, one launch (start us, length us, event | category | flops | bytes accessed | tf_op | source)
XLA Modules:
  0.0 119.7 jit_solution(1937072258397482137)
XLA Ops:
  0.6 0.9 copy.10
  1.6 0.7 reshape.7.refs_4_
  2.3 115.0 %shard_map.86 = (bf16[64,2048]{1,0:T(8,128)(2,1)}, f32[64,256]{1,0:T(8,128)}) custom-call(bf16[64,2048]{1,0:T(8,128)(2,1)} %refs_0_.1, bf16[64,64]{1,0:T(8,128)(2,1)} %refs_1_.1, f32[256]{0:T(256)} %refs_2_.1, s32[64,256]{1,0:T(8,128)} %refs_3_.1, s32[16,1024]{1,0:T(8,128)} %reshape.7.refs_4_, s32[1,512]{1,0:T(1,128)} %bitcast.7, f32[1,2048]{1,0:T(1,128)} %bitcast.5, ...), custom_call_target="tpu_custom_call" | custom-call | tf_op jit(solution)/shard_map/pallas_call | solution.py:262
  117.3 0.0 copy-start
  117.4 1.7 %copy.13 = bf16[64,2048]{1,0:T(8,128)(2,1)} copy(bf16[64,2048]{1,0:T(8,128)(2,1)} %get-tuple-element.4) | data formatting | bytes 524288
  119.1 0.0 copy-done
  119.1 0.6 copy.14
Async XLA Ops:
  117.3 1.7 %copy-start = (f32[64,256]{1,0:T(8,128)S(1)}, f32[64,256]{1,0:T(8,128)}, u32[]{:S(2)}) copy-start(f32[64,256]{1,0:T(8,128)} %get-tuple-element.5) | copy-start | bytes 196612

commit v6 on v5

--- a/solution.py
+++ b/solution.py
@@ -62,77 +62,107 @@
     lax.fori_loop(0, hots.shape[0], chunk, 0)
 
 
-def apply_cells(scaled, ghosts, hots, hots_t, part_of, scale, block, table, turned, spread, total):
-    rows, owned = scaled.shape
-    rim = ghosts.shape[-1]
-    height = table.shape[1]
-    corners = hots.shape[1] // CHUNK
-    count = hots.shape[0]
-    for at in range(0, owned, height):
-        row, col, width = place(at, owned, height, rows)
-        table[row : row + rows, col : col + width] = scaled[:, at : at + width]
-    for slot in range(len(OFFSETS)):
-        row, col, width = place(owned + slot * rim, rim, height, rows)
-        table[row : row + rows, col : col + width] = ghosts[slot]
-    turned[...] = table[...].astype(F32).T.astype(BF16)
-    lane = lax.broadcasted_iota(jnp.int32, (corners, 128), 1)
-    part_lane = [((lane + k) // rows).astype(F32).astype(BF16) for k in range(0, LANES, 128)]
-    left = lane < rows
-    per = DEPTH // corners
-    pairs = [(at + cell, at + per + cell) for at in range(0, CHUNK, 2 * per) for cell in range(per)]
-
-    def find(g):
-        return jnp.dot(hots[g], turned[...], preferred_element_type=F32)
-
-    def add(g):
-        total[...] += jnp.dot(hots_t[g], spread[...], preferred_element_type=F32)
-
-    def apply(g, found):
-        base = g * CHUNK
-
-        def mask(c):
-            part = part_of[g, c * corners : (c + 1) * corners, :]
-            return [jnp.where(part == lanes, 1.0, 0.0).astype(BF16) for lanes in part_lane]
-
-        def pick(c):
-            wide = found[c * corners : (c + 1) * corners].astype(BF16)
-            return sum(wide[:, k * 128 : (k + 1) * 128] * m for k, m in enumerate(mask(c))).astype(F32)
+class Cells:
+    def __init__(self, hots, hots_t, part_of, scale, block, turned, middle, total, rows, own_lanes):
+        self.hots, self.hots_t, self.part_of, self.scale, self.block = hots, hots_t, part_of, scale, block
+        self.turned, self.middle, self.total, self.rows = turned, middle, total, rows
+        self.own, self.ghost = (0, own_lanes), (own_lanes, LANES)
+        self.corners = hots.shape[1] // CHUNK
+        self.count = hots.shape[0]
+        self.lane = lax.broadcasted_iota(jnp.int32, (self.corners, 128), 1)
+
+    def mask(self, g, c, half):
+        part = self.part_of[g, c * self.corners : (c + 1) * self.corners, :]
+        for k in range(*half, 128):
+            yield jnp.where(part == ((self.lane + k) // self.rows).astype(F32).astype(BF16), 1.0, 0.0).astype(BF16)
+
+    def fill(self, half, pieces):
+        stacked = jnp.concatenate(pieces, axis=0)
+        self.turned[:, half[0] : half[1]] = stacked.astype(F32).T.astype(BF16)
+
+    def find(self, g, half):
+        return jnp.dot(self.hots[g], self.turned[:, half[0] : half[1]], preferred_element_type=F32)
+
+    def pick(self, g, c, found, half):
+        wide = found[c * self.corners : (c + 1) * self.corners].astype(BF16)
+        return sum(wide[:, k * 128 : (k + 1) * 128] * m for k, m in enumerate(self.mask(g, c, half)))
+
+    def gather_own(self):
+        def chunk(g, carry):
+            found = self.find(g, self.own)
+            for c in range(CHUNK):
+                self.middle[g, c * self.corners : (c + 1) * self.corners, :] = self.pick(g, c, found, self.own)
+            return carry
+
+        lax.fori_loop(0, self.count, chunk, 0)
+
+    def add(self, g, half):
+        spread = jnp.concatenate(
+            [
+                jnp.concatenate(
+                    [
+                        self.middle[g, c * self.corners : (c + 1) * self.corners, :] * m
+                        for m in self.mask(g, c, half)
+                    ],
+                    axis=1,
+                )
+                for c in range(CHUNK)
+            ],
+            axis=0,
+        )
+        self.total[:, half[0] : half[1]] += jnp.dot(self.hots_t[g], spread, preferred_element_type=F32)
+
+    def apply(self, g, found):
+        corners, rows, base = self.corners, self.rows, g * CHUNK
+        per = DEPTH // corners
+        left = self.lane < rows
+        pairs = [(at + cell, at + per + cell) for at in range(0, CHUNK, 2 * per) for cell in range(per)]
+
+        def whole(c):
+            earlier = self.middle[g, c * corners : (c + 1) * corners, :]
+            return (earlier + self.pick(g, c, found, self.ghost)).astype(F32)
 
         tiles = []
         for one, two in pairs:
-            first, other = pick(one), pick(two)
-            crossed = pltpu.roll(jnp.where(left, other, first), rows, axis=1)
-            tiles.append((jnp.where(left, first, other) + crossed).astype(BF16))
+            here, other = whole(one), whole(two)
+            crossed = pltpu.roll(jnp.where(left, other, here), rows, axis=1)
+            tiles.append((jnp.where(left, here, other) + crossed).astype(BF16))
         columns = [jnp.concatenate(tiles[at : at + per], axis=0) for at in range(0, len(tiles), per)]
-        term = jnp.dot(block[...], jnp.concatenate(columns, axis=1), preferred_element_type=F32)
+        term = jnp.dot(self.block[...], jnp.concatenate(columns, axis=1), preferred_element_type=F32)
         for k, (one, two) in enumerate(pairs):
             cell, column = k % per, k // per * 128
             tile = term[cell * corners : (cell + 1) * corners, column : column + 128]
-            tile = tile * jnp.where(left, scale[base + one], scale[base + two])
+            tile = tile * jnp.where(left, self.scale[base + one], self.scale[base + two])
             crossed = pltpu.roll(tile, rows, axis=1)
             for at, both in ((one, jnp.where(left, tile, crossed)), (two, jnp.where(left, crossed, tile))):
-                narrow = both.astype(BF16)
-                for n, m in enumerate(mask(at)):
-                    spread[at * corners : (at + 1) * corners, n * 128 : (n + 1) * 128] = narrow * m
-
-    total[...] = jnp.zeros_like(total)
-    apply(0, find(0))
-
-    def chunk(g, carry):
-        found = find(g)
-        add(g - 1)
-        apply(g, found)
-        return carry
-
-    lax.fori_loop(1, count, chunk, 0)
-    add(count - 1)
+                self.middle[g, at * corners : (at + 1) * corners, :] = both.astype(BF16)
+
+    def gather_ghosts_and_apply(self):
+        self.total[...] = jnp.zeros_like(self.total)
+        self.apply(0, self.find(0, self.ghost))
+
+        def chunk(g, carry):
+            found = self.find(g, self.ghost)
+            self.add(g - 1, self.ghost)
+            self.apply(g, found)
+            return carry
+
+        lax.fori_loop(1, self.count, chunk, 0)
+        self.add(self.count - 1, self.ghost)
+
+    def add_own(self):
+        def chunk(g, carry):
+            self.add(g, self.own)
+            return carry
+
+        lax.fori_loop(0, self.count, chunk, 0)
 
 
 def kernel(
     n_space, n_band,
     start, kinetic, scale, nodes, nodes_row, edge, potential, inv_root,
     filtered, margin,
-    hot, scaled, first, table, turned, total, block, hots, hots_t, part_of, spread, rims, ghosts, parts, back, quarters, gram, gram_in, gathered,
+    hot, scaled, first, turned, total, block, hots, hots_t, part_of, middle, rims, ghosts, parts, back, quarters, gram, gram_in, gathered,
     rim_send, rim_recv, part_send, part_recv, quarter_send, quarter_recv, gram_send, gram_recv, row_send, row_recv,
 ):
     p, b = lax.axis_index("space"), lax.axis_index("band")
@@ -151,7 +181,10 @@
 
     rows, owned = start.shape
     rim = edge.shape[-1]
-    height = table.shape[1]
+    height = turned.shape[0]
+    cells = Cells(
+        hots, hots_t, part_of, scale, block, turned, middle, total, rows, owned // height * rows
+    )
     corners = kinetic.shape[0]
     tiled = jnp.concatenate([kinetic[...].astype(F32)] * (DEPTH // corners), axis=0)
     tiled = jnp.concatenate([tiled] * (DEPTH // corners), axis=1)
@@ -174,11 +207,13 @@
         ]
         if turn == 0:
             build_hots(nodes, nodes_row, hots, hots_t, part_of, height)
+        cells.fill(cells.own, [scaled[:, at : at + height] for at in range(0, owned, height)])
+        cells.gather_own()
         for copy in sent:
             copy.wait()
-        apply_cells(
-            scaled, ghosts.at[turn], hots, hots_t, part_of, scale, block, table, turned, spread, total
-        )
+        joined = jnp.concatenate([ghosts[turn, slot] for slot in range(len(OFFSETS))], axis=1)
+        cells.fill(cells.ghost, [joined[:, at : at + height] for at in range(0, joined.shape[1], height)])
+        cells.gather_ghosts_and_apply()
         flipped = {}
 
         def piece(at, length):
@@ -197,6 +232,7 @@
                     space_at[offset % n_space],
                 )
             )
+        cells.add_own()
         own = jnp.concatenate([piece(at, owned) for at in range(0, owned, height)], axis=1)
         own = own + potential[...] * scaled[...].astype(F32)
         for copy in sent:
@@ -271,14 +307,13 @@
             pltpu.VMEM((owned, rim), BF16),
             pltpu.VMEM((rows, owned), BF16),
             pltpu.VMEM((rows, owned), BF16),
-            pltpu.VMEM((LANES, height), BF16),
             pltpu.VMEM((height, LANES), BF16),
             pltpu.VMEM((height, LANES), F32),
             pltpu.VMEM((DEPTH, DEPTH), BF16),
             pltpu.VMEM((count, step, height), BF16),
             pltpu.VMEM((count, height, step), BF16),
             pltpu.VMEM((count, step, 128), BF16),
-            pltpu.VMEM((step, LANES), BF16),
+            pltpu.VMEM((count, step, 128), BF16),
             pltpu.VMEM((2, rows, rim), BF16),
             pltpu.VMEM((2, slots, rows, rim), BF16),
             pltpu.VMEM((2, slots, rows, rim), BF16),
@@ -292,7 +327,7 @@
         + [pltpu.SemaphoreType.DMA((n_band,))] * 4
         + [pltpu.SemaphoreType.DMA((n_space,))] * 2,
         compiler_params=pltpu.CompilerParams(
-            collective_id=0, has_side_effects=True, vmem_limit_bytes=56 * 2**20
+            collective_id=0, has_side_effects=True, vmem_limit_bytes=58 * 2**20
         ),
     )(
         states_in, kinetic, cell_scale, cell_nodes, nodes_row,

time: 120 us -> 110 us (0.917)
  Pallas kernels: 115 us -> 105 us
    pallas_call x1, Pallas kernels: 115 us -> 105 us  [body(): pl.pallas_call(run, out_shape=(jax.ShapeDtypeStruct((rows, owned), BF16),...]
where the time goes in v6:
time: 110 us; the launch traced here: 109 us
  Pallas kernels  105 us (95%)
  local copies, waits for them, and re-layouts  4 us (4%)
    pallas_call x1, Pallas kernels, body(): pl.pallas_call(run, out_shape=(jax.ShapeDtypeStruct((rows, owned), BF16),...  105 us
    unnamed x4, local copies, waits for them, and re-layouts  2.33 us

profile of v6, /device:TPU:0, one launch (start us, length us, event | category | flops | bytes accessed | tf_op | source)
XLA Modules:
  0.0 109.4 jit_solution(2852931250454591081)
XLA Ops:
  0.6 0.9 copy.10
  1.6 0.7 reshape.7.refs_4_
  2.3 104.8 %shard_map.86 = (bf16[64,2048]{1,0:T(8,128)(2,1)}, f32[64,256]{1,0:T(8,128)}) custom-call(bf16[64,2048]{1,0:T(8,128)(2,1)} %refs_0_.1, bf16[64,64]{1,0:T(8,128)(2,1)} %refs_1_.1, f32[256]{0:T(256)} %refs_2_.1, s32[64,256]{1,0:T(8,128)} %refs_3_.1, s32[16,1024]{1,0:T(8,128)} %reshape.7.refs_4_, s32[1,512]{1,0:T(1,128)} %bitcast.7, f32[1,2048]{1,0:T(1,128)} %bitcast.5, ...), custom_call_target="tpu_custom_call" | custom-call | tf_op jit(solution)/shard_map/pallas_call | solution.py:298
  107.1 0.0 copy-start
  107.1 1.7 %copy.13 = bf16[64,2048]{1,0:T(8,128)(2,1)} copy(bf16[64,2048]{1,0:T(8,128)(2,1)} %get-tuple-element.4) | data formatting | bytes 524288
  108.8 0.0 copy-done
  108.8 0.6 copy.14
Async XLA Ops:
  107.1 1.7 %copy-start = (f32[64,256]{1,0:T(8,128)S(1)}, f32[64,256]{1,0:T(8,128)}, u32[]{:S(2)}) copy-start(f32[64,256]{1,0:T(8,128)} %get-tuple-element.5) | copy-start | bytes 196612
